TPU v7x, 256 devices: a whole 4x4x8 slice. The times are simulated.
256 devices in a mesh: dp: 64 (over x, z, core), tensor: 4 (over y).
Axes of the slice: x: 4, y: 4, z: 8, core: 2. Of those that a mesh axis runs over, the one named last changes fastest.
Arguments:
- queries: bfloat16 [24576, 8192], P('dp', 'tensor'), may hold values from -1100 to 1100
- keys: bfloat16 [24576, 1024], P('dp', 'tensor'), may hold values from -1100 to 1100
- values: bfloat16 [24576, 1024], P('dp', 'tensor'), may hold values from -6 to 6
- output_gradient: bfloat16 [24576, 8192], P('dp', 'tensor'), may hold values from -6 to 6
- q_gain: float32 [128], replicated, may hold values from 0.5 to 4.1
- k_gain: float32 [128], replicated, may hold values from 0.5 to 4.1
- prompt_len: int32 [64], P('dp'), may hold values from 1 to 256, as said below
- resp_len: int32 [128], P('dp'), may hold values from 1 to 64, as said below
- resp_owner: int32 [128], P('dp'), may hold values from 0 to 63, as said below
Outputs:
- q_grad: bfloat16 [24576, 8192], P('dp', 'tensor')
- k_grad: bfloat16 [24576, 1024], P('dp', 'tensor')
- v_grad: bfloat16 [24576, 1024], P('dp', 'tensor')
- q_gain_grad: float32 [128], replicated
- k_gain_grad: float32 [128], replicated
Inputs may be any that keep to these rules, and one draw needn't show every extreme that they name: `prompt_len`: some prompt has length exactly 256. `resp_len`: some response has length exactly 64. Response s lies on dp index floor(s / 2); that index minus resp_owner[s], modulo the number of dp indices, is 1 to 4, and equals 4 for some response.
All inputs are finite; a program needn't handle non-finite values.
Results may differ from a plain program's by a relative error of at most 0.009.
The roundings to bfloat16 on the way count: a program that leaves them out, or rounds other values in their place, can miss the bound.
Values may be sent and summed in bfloat16 or wider, within the bound.
A program may use at most 128 MiB of HBM per device.

v0:
```python
import jax
import jax.numpy as jnp
from jax import lax
from jax.sharding import PartitionSpec as P

PROMPT_LENGTH = 256
RESPONSE_LENGTH = 64
REACH = 4


EPSILON = 1e-06


def passed_along(block, axis, distance):
    devices = range(lax.axis_size(axis))
    route = [((i - distance) % len(devices), i) for i in devices]
    return lax.ppermute(block, axis, route)


def normalize(source, gain_vec):
    widened = source.astype(jnp.float32)
    inverse = lax.rsqrt(jnp.mean(widened * widened, axis=-1, keepdims=True) + EPSILON)
    return ((widened * inverse * gain_vec).astype(jnp.bfloat16), inverse)


def norm_backward(upstream, source, inverse, gain_vec):
    widened = source.astype(jnp.float32)
    scaled = upstream * gain_vec
    mean_term = jnp.mean(scaled * widened, axis=-1, keepdims=True)
    result = inverse * scaled - widened * inverse**3 * mean_term
    gain_part = jnp.sum((upstream * widened * inverse).reshape(-1, widened.shape[-1]), axis=0)
    return (result, gain_part)


def attend(q_rows, k_rows, v_rows, d_rows, allowed):
    score_scale = q_rows.shape[-1] ** (-0.5)
    scores = (
        jnp.einsum("mgd,nd->gmn", q_rows, k_rows, preferred_element_type=jnp.float32) * score_scale
    )
    scores = jnp.where(allowed[None], scores, -jnp.inf)
    row_max = jnp.max(scores, axis=-1, keepdims=True)
    raised = jnp.exp(scores - row_max)
    probability = raised / jnp.sum(raised, axis=-1, keepdims=True)
    weights = probability.astype(jnp.bfloat16)
    output = jnp.einsum("gmn,nd->mgd", weights, v_rows, preferred_element_type=jnp.float32)
    v_grad = jnp.einsum("gmn,mgd->nd", weights, d_rows, preferred_element_type=jnp.float32)
    p_grad = jnp.einsum("mgd,nd->gmn", d_rows, v_rows, preferred_element_type=jnp.float32)
    row_inner = jnp.einsum(
        "mgd,mgd->gm", d_rows.astype(jnp.float32), output, precision=lax.Precision.HIGHEST
    )[..., None]
    s_grad = (probability * (p_grad - row_inner) * score_scale).astype(jnp.bfloat16)
    q_grad = jnp.einsum("gmn,nd->mgd", s_grad, k_rows, preferred_element_type=jnp.float32)
    k_grad = jnp.einsum("gmn,mgd->nd", s_grad, q_rows, preferred_element_type=jnp.float32)
    return (q_grad, k_grad, v_grad)


def on_device(
    queries, keys, values, output_gradient, q_gain, k_gain, prompt_len, resp_len, resp_owner
):
    head_dim = q_gain.shape[0]
    overall_rows = queries.shape[0]
    kv_heads = keys.shape[1] // head_dim
    query_group_size = queries.shape[1] // keys.shape[1]
    slot_total_count = resp_len.shape[0]
    device = lax.axis_index("dp")
    cycle_size = lax.axis_size("dp")
    query_unnormed = queries.reshape(overall_rows, kv_heads, query_group_size, head_dim)
    key_unnormed = keys.reshape(overall_rows, kv_heads, head_dim)
    value_row_block = values.reshape(overall_rows, kv_heads, head_dim)
    query_head_norm, query_inv = normalize(query_unnormed, q_gain)
    key_head_norm, key_inv = normalize(key_unnormed, k_gain)
    prompt_keep = jnp.arange(PROMPT_LENGTH) < prompt_len[0]
    reply_keep = (jnp.arange(RESPONSE_LENGTH)[None, :] < resp_len[:, None]).reshape(-1)
    row_keep_mask = jnp.concatenate([prompt_keep, reply_keep])
    gradient_rows = jnp.where(
        row_keep_mask[:, None, None, None],
        output_gradient.reshape(overall_rows, kv_heads, query_group_size, head_dim),
        jnp.zeros((), jnp.bfloat16),
    )
    causal = jnp.arange(PROMPT_LENGTH)[None, :] <= jnp.arange(PROMPT_LENGTH)[:, None]
    prompt_mask = causal & prompt_keep[None, :]

    def prompt_head(inputs):
        return attend(inputs[0], inputs[1], inputs[2], inputs[3], prompt_mask)

    head_first = (
        jnp.moveaxis(query_head_norm[:PROMPT_LENGTH], 1, 0),
        jnp.moveaxis(key_head_norm[:PROMPT_LENGTH], 1, 0),
        jnp.moveaxis(value_row_block[:PROMPT_LENGTH], 1, 0),
        jnp.moveaxis(gradient_rows[:PROMPT_LENGTH], 1, 0),
    )
    prompt_query_gradient, prompt_key_gradient, prompt_value_gradient = lax.map(
        prompt_head, head_first
    )
    prompt_query_gradient = jnp.moveaxis(prompt_query_gradient, 0, 1)
    prompt_key_gradient = jnp.moveaxis(prompt_key_gradient, 0, 1)
    prompt_value_gradient = jnp.moveaxis(prompt_value_gradient, 0, 1)
    own_keys = key_head_norm[:PROMPT_LENGTH]
    own_values = value_row_block[:PROMPT_LENGTH]
    key_list = []
    value_list = []
    length_list = []
    for offset in range(1, REACH + 1):
        got_keys, got_values, got_length = passed_along(
            (own_keys, own_values, prompt_len), "dp", offset
        )
        key_list.append(got_keys)
        value_list.append(got_values)
        length_list.append(got_length)
    fetched_keys = jnp.stack(key_list)
    fetched_values = jnp.stack(value_list)
    fetched_length = jnp.concatenate(length_list)
    pick_index = (device - resp_owner) % cycle_size - 1
    choose = pick_index[:, None] == jnp.arange(REACH)[None, :]
    owner_length = jnp.sum(jnp.where(choose, fetched_length[None, :], 0), axis=1)
    slot_keys = jnp.take(fetched_keys, pick_index, axis=0)
    slot_values = jnp.take(fetched_values, pick_index, axis=0)
    response_queries = query_head_norm[PROMPT_LENGTH:].reshape(
        slot_total_count, RESPONSE_LENGTH, kv_heads, query_group_size, head_dim
    )
    response_keys = key_head_norm[PROMPT_LENGTH:].reshape(
        slot_total_count, RESPONSE_LENGTH, kv_heads, head_dim
    )
    response_values = value_row_block[PROMPT_LENGTH:].reshape(
        slot_total_count, RESPONSE_LENGTH, kv_heads, head_dim
    )
    response_output_gradient = gradient_rows[PROMPT_LENGTH:].reshape(
        slot_total_count, RESPONSE_LENGTH, kv_heads, query_group_size, head_dim
    )
    all_keys = jnp.concatenate([slot_keys, response_keys], axis=1)
    all_values = jnp.concatenate([slot_values, response_values], axis=1)
    prompt_part = jnp.arange(PROMPT_LENGTH)[None, None, :] < owner_length[:, None, None]
    own_part = jnp.arange(RESPONSE_LENGTH)[None, :] <= jnp.arange(RESPONSE_LENGTH)[:, None]
    reply_mask = jnp.concatenate(
        [
            jnp.broadcast_to(prompt_part, (slot_total_count, RESPONSE_LENGTH, PROMPT_LENGTH)),
            jnp.broadcast_to(own_part[None], (slot_total_count, RESPONSE_LENGTH, RESPONSE_LENGTH)),
        ],
        axis=2,
    )
    per_head = jax.vmap(attend, in_axes=(1, 1, 1, 1, None), out_axes=(1, 1, 1))
    per_slot = jax.vmap(per_head, in_axes=(0, 0, 0, 0, 0))
    response_query_gradient, response_key_gradient, response_value_gradient = per_slot(
        response_queries, all_keys, all_values, response_output_gradient, reply_mask
    )
    choose_real = choose.astype(jnp.float32).T
    back_keys = jnp.sum(
        choose_real[:, :, None, None, None] * response_key_gradient[None, :, :PROMPT_LENGTH], axis=1
    )
    back_values = jnp.sum(
        choose_real[:, :, None, None, None] * response_value_gradient[None, :, :PROMPT_LENGTH],
        axis=1,
    )
    key_total = prompt_key_gradient
    value_total = prompt_value_gradient
    for offset in range(1, REACH + 1):
        got_keys, got_values = (
            passed_along(back_keys[offset - 1].astype(jnp.bfloat16), "dp", -offset).astype(
                jnp.float32
            ),
            passed_along(back_values[offset - 1].astype(jnp.bfloat16), "dp", -offset).astype(
                jnp.float32
            ),
        )
        key_total = key_total + got_keys
        value_total = value_total + got_values
    key_row_block = jnp.concatenate(
        [key_total, response_key_gradient[:, PROMPT_LENGTH:].reshape(-1, kv_heads, head_dim)]
    )
    value_running_sums = jnp.concatenate(
        [value_total, response_value_gradient[:, PROMPT_LENGTH:].reshape(-1, kv_heads, head_dim)]
    )
    query_row_block = jnp.concatenate(
        [
            prompt_query_gradient,
            response_query_gradient.reshape(-1, kv_heads, query_group_size, head_dim),
        ]
    )
    query_backward, query_portion = norm_backward(
        query_row_block, query_unnormed, query_inv, q_gain
    )
    key_backward, key_portion = norm_backward(key_row_block, key_unnormed, key_inv, k_gain)
    q_gain_grad, k_gain_grad = lax.psum((query_portion, key_portion), ("dp", "tensor"))
    return (
        query_backward.reshape(overall_rows, -1).astype(jnp.bfloat16),
        key_backward.reshape(overall_rows, -1).astype(jnp.bfloat16),
        value_running_sums.reshape(overall_rows, -1).astype(jnp.bfloat16),
        q_gain_grad,
        k_gain_grad,
    )


def solution(mesh):
    placed = (
        P("dp", "tensor"),
        P("dp", "tensor"),
        P("dp", "tensor"),
        P("dp", "tensor"),
        P(),
        P(),
        P("dp"),
        P("dp"),
        P("dp"),
    )
    return jax.shard_map(
        on_device,
        mesh=mesh,
        in_specs=placed,
        out_specs=(P("dp", "tensor"), P("dp", "tensor"), P("dp", "tensor"), P(), P()),
        check_vma=False,
    )
```

profile of v0, /device:TPU:1, one launch (start us, length us, event | category | flops | bytes accessed | tf_op | source)
XLA Modules:
  0.0 237.8 jit_solution(5137738660719563027)
XLA Ops:
  2.4 3.8 %collective-permute-start.11 = (bf16[256,2,128]{2,0,1:T(8,128)(2,1)}, bf16[256,2,128]{2,0,1:T(8,128)(2,1)}, u32[]{:S(2)}, u32[]{:S(2)}) collective-permute-start(bf16[256,2,128]{2,0,1:T(8,128)(2,1)} %copy.253), channel_id=1, source_target_pairs={{240,0},{244,4},{248,8},{252,12},{0,16},{4,20},{8,24},{12,28},{16,... | collective-permute-start | bytes 393224 | tf_op jit(solution)/shard_map/ppermute | solution.py:17
  6.2 5.0 %collective-permute-start.10 = (bf16[256,2,128]{2,0,1:T(8,128)(2,1)}, bf16[256,2,128]{2,0,1:T(8,128)(2,1)}, u32[]{:S(2)}, u32[]{:S(2)}) collective-permute-start(bf16[256,2,128]{2,0,1:T(8,128)(2,1)} %copy.253), channel_id=1, source_target_pairs={{244,0},{248,4},{252,8},{0,12},{4,16},{8,20},{12,24},{16,28},{20,3... | collective-permute-start | bytes 393224 | tf_op jit(solution)/shard_map/ppermute | solution.py:17
  12.1 1.3 collective-permute-start.7
  14.1 1.8 convert_bitcast_fusion
  16.6 1.3 multiply_reduce_fusion
  18.6 1.4 multiply_multiply_fusion
  19.9 0.9 copy.242
  20.9 1.0 multiply_convert_fusion
  25.5 1.9 copy.246
  29.5 31.3 %while.15 = (s32[]{:T(128)}, f32[2,256,8,128]{3,2,0,1:T(8,128)}, f32[2,256,128]{2,1,0:T(8,128)}, f32[2,256,128]{2,1,0:T(8,128)}, bf16[2,256,128]{2,1,0:T(8,128)(...) while((s32[]{:T(128)}, f32[2,256,8,128]{3,2,0,1:T(8,128)}, ...), condition=%wide.region_5.6_spmd.clone, body=%wide.region_2.5_spmd.clone.sunk | while | flops 813037824 | bytes 66833252 | solution.py:92
  32.0 3.2 %fusion.126 = (f32[8,256]{1,0:T(8,128)S(1)}, f32[8,256,256]{1,2,0:T(8,128)}) fusion(pred[256,256]{0,1:T(8,128)(4,1)S(1)} %fusion.125, bf16[1,256,8,128]{3,2,0,1:T(8,128)(2,1)S(1)} %constant_dynamic-slice_fusion.7, bf16[2,256,128]{2,1,0:T(8,128)(2,1)} %get-tuple-element.316, s32[]{:T(128)S(6)} %copy.378), kind=kOutput, calls=%fused_computation.171.clone.1 | convolution fusion | flops 136315136 | bytes 2760708 | tf_op jit(solution)/shard_map/while/body/eval_jaxpr/sub | solution.py:42
  35.8 2.1 fusion.127
  38.4 1.2 fusion.128
  40.4 1.1 constant_dynamic-update-slice_fusion.3
  42.3 2.1 fusion.130
  47.6 3.2 %fusion.126 = (f32[8,256]{1,0:T(8,128)S(1)}, f32[8,256,256]{1,2,0:T(8,128)}) fusion(pred[256,256]{0,1:T(8,128)(4,1)S(1)} %fusion.125, bf16[1,256,8,128]{3,2,0,1:T(8,128)(2,1)S(1)} %constant_dynamic-slice_fusion.7, bf16[2,256,128]{2,1,0:T(8,128)(2,1)} %get-tuple-element.316, s32[]{:T(128)S(6)} %copy.378), kind=kOutput, calls=%fused_computation.171.clone.1 | convolution fusion | flops 136315136 | bytes 2760708 | tf_op jit(solution)/shard_map/while/body/eval_jaxpr/sub | solution.py:42
  51.4 2.1 fusion.127
  54.0 1.2 fusion.128
  56.1 1.1 constant_dynamic-update-slice_fusion.3
  57.9 2.1 fusion.130
  60.8 3.9 %bitcast_dynamic-update-slice_fusion = f32[384,2048]{1,0:T(8,128)} fusion(f32[32,8,16,128]{3,2,1,0:T(8,128)} %bitcast.305), kind=kLoop, calls=%fused_computation.73 | loop fusion | bytes 4194304
  68.5 6.0 %collective-permute-done.6 = s32[1]{0:T(128)} collective-permute-done((s32[1]{0:T(128)}, s32[1]{0:T(128)}, u32[]{:S(2)}, u32[]{:S(2)}) %collective-permute-start.6) | collective-permute-done | bytes 36 | tf_op jit(solution)/shard_map/ppermute | solution.py:17
  74.5 5.8 %collective-permute-done.5 = s32[1]{0:T(128)} collective-permute-done((s32[1]{0:T(128)}, s32[1]{0:T(128)}, u32[]{:S(2)}, u32[]{:S(2)}) %collective-permute-start.5) | collective-permute-done | bytes 36 | tf_op jit(solution)/shard_map/ppermute | solution.py:17
  80.3 3.7 %collective-permute-done.4 = s32[1]{0:T(128)} collective-permute-done((s32[1]{0:T(128)}, s32[1]{0:T(128)}, u32[]{:S(2)}, u32[]{:S(2)}) %collective-permute-start.4) | collective-permute-done | bytes 36 | tf_op jit(solution)/shard_map/ppermute | solution.py:17
  84.1 2.5 %pad_add_fusion.2 = s32[4]{0:T(128)S(1)} fusion(s32[1]{0:T(128)} %collective-permute-done.7, s32[1]{0:T(128)} %collective-permute-done.6, s32[1]{0:T(128)} %collective-permute-done.5, s32[1]{0:T(128)} %collective-permute-done.4), kind=kLoop, calls=%fused_computation.160 | loop fusion | flops 12 | bytes 32 | tf_op jit(solution)/shard_map/concatenate | solution.py:112
  86.9 1.8 collective-permute-start.2
  90.0 1.2 pad_maximum_fusion.1
  91.9 4.1 %collective-permute-done.3 = bf16[256,2,128]{2,0,1:T(8,128)(2,1)} collective-permute-done((bf16[256,2,128]{2,0,1:T(8,128)(2,1)S(1)}, bf16[256,2,128]{2,0,1:T(8,128)(2,1)}, u32[]{:S(2)}, u32[]{:S(2)}) %collective-permute-start.3) | collective-permute-done | bytes 131104 | tf_op jit(solution)/shard_map/ppermute | solution.py:17
  96.7 5.2 %collective-permute-done.1 = bf16[256,2,128]{2,0,1:T(8,128)(2,1)} collective-permute-done((bf16[256,2,128]{2,0,1:T(8,128)(2,1)S(1)}, bf16[256,2,128]{2,0,1:T(8,128)(2,1)}, u32[]{:S(2)}, u32[]{:S(2)}) %collective-permute-start.1) | collective-permute-done | bytes 131104 | tf_op jit(solution)/shard_map/ppermute | solution.py:17
  101.9 1.2 pad_maximum_fusion
  104.6 1.4 fusion.64
  106.0 1.4 fusion.90
  109.1 0.9 fusion.53
  110.6 1.6 convolution_bitcast_fusion.7
  112.2 1.6 convolution_bitcast_fusion.6
  113.7 1.6 copy.260
  115.3 2.3 concatenate.52
  117.6 3.8 %fusion.50 = f32[384,2,8]{2,1,0:T(2,128)} fusion(f32[384,2,8,128]{3,2,1,0:T(8,128)S(1)} %bitcast.300, f32[128,2,8,128]{3,2,1,0:T(8,128)} %bitcast.304, f32[256,2,8,128]{3,2,1,0:T(8,128)} %bitcast.306, f32[128]{0:T(128)S(1)} %copy-done.51), kind=kLoop, calls=%fused_computation.63 | loop fusion | flops 3139584 | bytes 6316544 | tf_op jit(solution)/shard_map/reduce_sum | solution.py:29
  121.4 1.2 copy.263
  123.4 3.8 %collective-permute-start.19 = (bf16[256,2,128]{2,0,1:T(8,128)(2,1)S(1)}, bf16[256,2,128]{2,0,1:T(8,128)(2,1)S(1)}, u32[]{:S(2)}, u32[]{:S(2)}) collective-permute-start(bf16[256,2,128]{2,0,1:T(8,128)(2,1)S(1)} %get-tuple-element.216), channel_id=1, source_target_pairs={{16,0},{20,4},{24,8},{28,12},{32,16},{36,20},{40,24},{44,28},{48,3... | collective-permute-start | bytes 393224 | tf_op jit(solution)/shard_map/ppermute | solution.py:17
  127.1 1.5 collective-permute-start.18
  128.7 1.6 collective-permute-start.17
  131.2 9.7 %collective-permute-start.14 = (bf16[256,2,128]{2,0,1:T(8,128)(2,1)S(1)}, bf16[256,2,128]{2,0,1:T(8,128)(2,1)}, u32[]{:S(2)}, u32[]{:S(2)}) collective-permute-start(bf16[256,2,128]{2,0,1:T(8,128)(2,1)S(1)} %get-tuple-element.218), channel_id=1, source_target_pairs={{12,0},{16,4},{20,8},{24,12},{28,16},{32,20},{36,24},{40,28},{44,3... | collective-permute-start | bytes 393224 | tf_op jit(solution)/shard_map/ppermute | solution.py:17
  140.9 2.3 collective-permute-start.13
  148.0 5.6 %fusion.48 = (f32[2048]{0:T(1024)S(1)}, bf16[384,2048]{1,0:T(8,128)(2,1)}) fusion(f32[384,2048]{1,0:T(8,128)S(1)} %constant_dynamic-update-slice_fusion.1, bf16[384,2048]{1,0:T(8,128)(2,1)S(1)} %copy-done.10, f32[48,8,16,128]{3,2,1,0:T(8,128)S(1)} %bitcast.301, f32[48,8,16,128]{3,2,1,0:T(8,128)S(1)} %bitcast.302, f32[48,8,16,128]{3,2,1,0:T(8,128)S(1)} %bitcast.303, ...), kind=kLoop, calls=%fused_computation.59 | loop fusion | flops 7862272 | bytes 15745024 | tf_op jit(solution)/shard_map/reduce_sum | solution.py:31
  154.3 1.3 collective-permute-done.12
  155.7 1.3 fusion.74
  159.4 78.2 %all-reduce = (f32[128]{0:T(128)}, f32[128]{0:T(128)}) all-reduce(f32[128]{0:T(128)S(1)} %bitcast_reduce_fusion, f32[128]{0:T(128)S(1)} %bitcast_reduce_fusion.1), channel_id=1, replica_groups=mesh['dp'=64,'tensor'=4] {'dp','tensor'}, use_global_device_ids=true, to_apply=%region_15.17 | all-reduce | flops 256 | bytes 2048 | tf_op jit(solution)/shard_map/psum | solution.py:183
  (277 shorter events, 40.8 us)
Async XLA Ops:
  1.7 12.4 %copy-start.23 = (bf16[256,256]{0,1:T(8,128)(2,1)}, bf16[256,256]{0,1:T(8,128)(2,1)S(1)}, u32[]{:S(2)}) copy-start(bf16[256,256]{0,1:T(8,128)(2,1)S(1)} %copy.310) | copy-start | bytes 393220
  2.4 84.4 %collective-permute-start.11 = (bf16[256,2,128]{2,0,1:T(8,128)(2,1)}, bf16[256,2,128]{2,0,1:T(8,128)(2,1)}, u32[]{:S(2)}, u32[]{:S(2)}) collective-permute-start(bf16[256,2,128]{2,0,1:T(8,128)(2,1)} %copy.253), channel_id=1, source_target_pairs={{240,0},{244,4},{248,8},{252,12},{0,16},{4,20},{8,24},{12,28},{16,... | collective-permute-start | bytes 393224 | tf_op jit(solution)/shard_map/ppermute | solution.py:17
  6.2 82.5 %collective-permute-start.10 = (bf16[256,2,128]{2,0,1:T(8,128)(2,1)}, bf16[256,2,128]{2,0,1:T(8,128)(2,1)}, u32[]{:S(2)}, u32[]{:S(2)}) collective-permute-start(bf16[256,2,128]{2,0,1:T(8,128)(2,1)} %copy.253), channel_id=1, source_target_pairs={{244,0},{248,4},{252,8},{0,12},{4,16},{8,20},{12,24},{16,28},{20,3... | collective-permute-start | bytes 393224 | tf_op jit(solution)/shard_map/ppermute | solution.py:17
  11.3 77.9 %collective-permute-start.9 = (bf16[256,2,128]{2,0,1:T(8,128)(2,1)}, bf16[256,2,128]{2,0,1:T(8,128)(2,1)}, u32[]{:S(2)}, u32[]{:S(2)}) collective-permute-start(bf16[256,2,128]{2,0,1:T(8,128)(2,1)} %copy.253), channel_id=1, source_target_pairs={{248,0},{252,4},{0,8},{4,12},{8,16},{12,20},{16,24},{20,28},{24,32... | collective-permute-start | bytes 393224 | tf_op jit(solution)/shard_map/ppermute | solution.py:17
  12.0 78.0 %collective-permute-start.8 = (bf16[256,2,128]{2,0,1:T(8,128)(2,1)}, bf16[256,2,128]{2,0,1:T(8,128)(2,1)}, u32[]{:S(2)}, u32[]{:S(2)}) collective-permute-start(bf16[256,2,128]{2,0,1:T(8,128)(2,1)} %copy.253), channel_id=1, source_target_pairs={{252,0},{0,4},{4,8},{8,12},{12,16},{16,20},{20,24},{24,28},{28,32}... | collective-permute-start | bytes 393224 | tf_op jit(solution)/shard_map/ppermute | solution.py:17
  12.1 55.9 %collective-permute-start.7 = (s32[1]{0:T(128)}, s32[1]{0:T(128)}, u32[]{:S(2)}, u32[]{:S(2)}) collective-permute-start(s32[1]{0:T(128)} %param.19), channel_id=1, source_target_pairs={{240,0},{244,4},{248,8},{252,12},{0,16},{4,20},{8,24},{12,28},{16,... | collective-permute-start | bytes 20 | tf_op jit(solution)/shard_map/ppermute | solution.py:17
  16.5 4.3 %copy-start = (f32[48,8,16,128]{3,2,1,0:T(8,128)}, f32[48,8,16,128]{3,2,1,0:T(8,128)S(1)}, u32[]{:S(2)}) copy-start(f32[48,8,16,128]{3,2,1,0:T(8,128)S(1)} %copy.325) | copy-start | bytes 9437188
  16.5 4.3 %copy-start.49 = (f32[128]{0:T(128)S(1)}, f32[128]{0:T(128)}, u32[]{:S(2)}) copy-start(f32[128]{0:T(128)} %param.17) | copy-start | bytes 1540
  32.0 3.8 %copy-start.24 = (bf16[2,256,128]{1,2,0:T(8,128)(2,1)S(1)}, bf16[2,256,128]{1,2,0:T(8,128)(2,1)}, u32[]{:S(2)}) copy-start(bf16[2,256,128]{1,2,0:T(8,128)(2,1)} %get-tuple-element.318) | copy-start | bytes 393220 | tf_op jit(solution)/shard_map/while
  47.6 3.8 %copy-start.24 = (bf16[2,256,128]{1,2,0:T(8,128)(2,1)S(1)}, bf16[2,256,128]{1,2,0:T(8,128)(2,1)}, u32[]{:S(2)}) copy-start(bf16[2,256,128]{1,2,0:T(8,128)(2,1)} %get-tuple-element.318) | copy-start | bytes 393220 | tf_op jit(solution)/shard_map/while
  60.8 3.9 %copy-start.55 = (s32[2]{0:T(128)S(1)}, s32[2]{0:T(128)}, u32[]{:S(2)}) copy-start(s32[2]{0:T(128)} %param.21) | copy-start | bytes 28
  60.8 4.4 %slice-start = ((bf16[384,2,8,128]{0,3,2,1:T(8,128)(2,1)}), bf16[128,2,8,128]{0,3,2,1:T(8,128)(2,1)S(1)}, s32[]{:S(2)}) async-start(bf16[384,2,8,128]{0,3,2,1:T(8,128)(2,1)} %copy-done.11), calls=%async_computation | async-start | bytes 1048576 | tf_op jit(solution)/shard_map/slice | solution.py:127
  64.7 19.3 %copy-start.34 = (bf16[256,2,128]{2,0,1:T(8,128)(2,1)S(1)}, bf16[256,2,128]{2,0,1:T(8,128)(2,1)}, u32[]{:S(2)}) copy-start(bf16[256,2,128]{2,0,1:T(8,128)(2,1)} %get-tuple-element.222) | copy-start | bytes 393220
  65.2 26.1 %copy-start.48 = (s32[1024]{0:T(1024)}, s32[1024]{0:T(1024)S(1)}, u32[]{:S(2)}) copy-start(s32[1024]{0:T(1024)S(1)} %pad_clamp_fusion) | copy-start | bytes 12292
  67.9 6.5 %collective-permute-start.6 = (s32[1]{0:T(128)}, s32[1]{0:T(128)}, u32[]{:S(2)}, u32[]{:S(2)}) collective-permute-start(s32[1]{0:T(128)} %param.19), channel_id=1, source_target_pairs={{244,0},{248,4},{252,8},{0,12},{4,16},{8,20},{12,24},{16,28},{20,3... | collective-permute-start | bytes 20 | tf_op jit(solution)/shard_map/ppermute | solution.py:17
  74.5 5.8 %collective-permute-start.5 = (s32[1]{0:T(128)}, s32[1]{0:T(128)}, u32[]{:S(2)}, u32[]{:S(2)}) collective-permute-start(s32[1]{0:T(128)} %param.19), channel_id=1, source_target_pairs={{248,0},{252,4},{0,8},{4,12},{8,16},{12,20},{16,24},{20,28},{24,32... | collective-permute-start | bytes 20 | tf_op jit(solution)/shard_map/ppermute | solution.py:17
  80.2 3.7 %collective-permute-start.4 = (s32[1]{0:T(128)}, s32[1]{0:T(128)}, u32[]{:S(2)}, u32[]{:S(2)}) collective-permute-start(s32[1]{0:T(128)} %param.19), channel_id=1, source_target_pairs={{252,0},{0,4},{4,8},{8,12},{12,16},{16,20},{20,24},{24,28},{28,32}... | collective-permute-start | bytes 20 | tf_op jit(solution)/shard_map/ppermute | solution.py:17
  83.9 12.0 %collective-permute-start.3 = (bf16[256,2,128]{2,0,1:T(8,128)(2,1)S(1)}, bf16[256,2,128]{2,0,1:T(8,128)(2,1)}, u32[]{:S(2)}, u32[]{:S(2)}) collective-permute-start(bf16[256,2,128]{2,0,1:T(8,128)(2,1)S(1)} %copy-done.34), channel_id=1, source_target_pairs={{240,0},{244,4},{248,8},{252,12},{0,16},{4,20},{8,24},{12,28},{16,... | collective-permute-start | bytes 393224 | tf_op jit(solution)/shard_map/ppermute | solution.py:17
  86.9 9.9 %collective-permute-start.2 = (bf16[256,2,128]{2,0,1:T(8,128)(2,1)S(1)}, bf16[256,2,128]{2,0,1:T(8,128)(2,1)}, u32[]{:S(2)}, u32[]{:S(2)}) collective-permute-start(bf16[256,2,128]{2,0,1:T(8,128)(2,1)S(1)} %copy-done.34), channel_id=1, source_target_pairs={{244,0},{248,4},{252,8},{0,12},{4,16},{8,20},{12,24},{16,28},{20,3... | collective-permute-start | bytes 393224 | tf_op jit(solution)/shard_map/ppermute | solution.py:17
  88.7 13.2 %collective-permute-start.1 = (bf16[256,2,128]{2,0,1:T(8,128)(2,1)S(1)}, bf16[256,2,128]{2,0,1:T(8,128)(2,1)}, u32[]{:S(2)}, u32[]{:S(2)}) collective-permute-start(bf16[256,2,128]{2,0,1:T(8,128)(2,1)S(1)} %copy-done.34), channel_id=1, source_target_pairs={{248,0},{252,4},{0,8},{4,12},{8,16},{12,20},{16,24},{20,28},{24,32... | collective-permute-start | bytes 393224 | tf_op jit(solution)/shard_map/ppermute | solution.py:17
  89.2 12.8 %collective-permute-start = (bf16[256,2,128]{2,0,1:T(8,128)(2,1)S(1)}, bf16[256,2,128]{2,0,1:T(8,128)(2,1)}, u32[]{:S(2)}, u32[]{:S(2)}) collective-permute-start(bf16[256,2,128]{2,0,1:T(8,128)(2,1)S(1)} %copy-done.34), channel_id=1, source_target_pairs={{252,0},{0,4},{4,8},{8,12},{12,16},{16,20},{20,24},{24,28},{28,32}... | collective-permute-start | bytes 393224 | tf_op jit(solution)/shard_map/ppermute | solution.py:17
  90.0 14.6 %copy-start.12 = (bf16[128,2,8,128]{3,2,1,0:T(8,128)(2,1)S(1)}, bf16[128,2,8,128]{3,2,1,0:T(8,128)(2,1)}, u32[]{:S(2)}) copy-start(bf16[128,2,8,128]{3,2,1,0:T(8,128)(2,1)} %slice.104) | copy-start | bytes 1572868
  113.7 3.9 %copy-start.1 = (f32[48,8,16,128]{3,2,1,0:T(8,128)S(1)}, f32[48,8,16,128]{3,2,1,0:T(8,128)}, u32[]{:S(2)}) copy-start(f32[48,8,16,128]{3,2,1,0:T(8,128)} %copy-done) | copy-start | bytes 9437188
  113.7 3.9 %copy-start.51 = (f32[128]{0:T(128)S(1)}, f32[128]{0:T(128)}, u32[]{:S(2)}) copy-start(f32[128]{0:T(128)} %param.17) | copy-start | bytes 1540
  122.9 7.5 %copy-start.9 = (f32[384,2048]{1,0:T(8,128)S(1)}, f32[384,2048]{1,0:T(8,128)}, u32[]{:S(2)}) copy-start(f32[384,2048]{1,0:T(8,128)} %bitcast_dynamic-update-slice_fusion) | copy-start | bytes 9437188
  122.9 7.5 %copy-start.13 = (f32[128,2048]{1,0:T(8,128)S(1)}, f32[128,2048]{1,0:T(8,128)}, u32[]{:S(2)}) copy-start(f32[128,2048]{1,0:T(8,128)} %concatenate.52) | copy-start | bytes 3145732
  123.3 21.4 %copy-start.15 = (f32[384,2,8]{2,1,0:T(2,128)S(1)}, f32[384,2,8]{2,1,0:T(2,128)}, u32[]{:S(2)}) copy-start(f32[384,2,8]{2,1,0:T(2,128)} %copy-done.14) | copy-start | bytes 73732
  123.4 7.8 %collective-permute-start.19 = (bf16[256,2,128]{2,0,1:T(8,128)(2,1)S(1)}, bf16[256,2,128]{2,0,1:T(8,128)(2,1)S(1)}, u32[]{:S(2)}, u32[]{:S(2)}) collective-permute-start(bf16[256,2,128]{2,0,1:T(8,128)(2,1)S(1)} %get-tuple-element.216), channel_id=1, source_target_pairs={{16,0},{20,4},{24,8},{28,12},{32,16},{36,20},{40,24},{44,28},{48,3... | collective-permute-start | bytes 393224 | tf_op jit(solution)/shard_map/ppermute | solution.py:17
  127.1 13.8 %collective-permute-start.18 = (bf16[256,2,128]{2,0,1:T(8,128)(2,1)S(1)}, bf16[256,2,128]{2,0,1:T(8,128)(2,1)S(1)}, u32[]{:S(2)}, u32[]{:S(2)}) collective-permute-start(bf16[256,2,128]{2,0,1:T(8,128)(2,1)S(1)} %get-tuple-element.214), channel_id=1, source_target_pairs={{12,0},{16,4},{20,8},{24,12},{28,16},{32,20},{36,24},{40,28},{44,3... | collective-permute-start | bytes 393224 | tf_op jit(solution)/shard_map/ppermute | solution.py:17
  128.7 14.6 %collective-permute-start.17 = (bf16[256,2,128]{2,0,1:T(8,128)(2,1)S(1)}, bf16[256,2,128]{2,0,1:T(8,128)(2,1)S(1)}, u32[]{:S(2)}, u32[]{:S(2)}) collective-permute-start(bf16[256,2,128]{2,0,1:T(8,128)(2,1)S(1)} %get-tuple-element.215), channel_id=1, source_target_pairs={{8,0},{12,4},{16,8},{20,12},{24,16},{28,20},{32,24},{36,28},{40,32... | collective-permute-start | bytes 393224 | tf_op jit(solution)/shard_map/ppermute | solution.py:17
  130.3 24.0 %collective-permute-start.16 = (bf16[256,2,128]{2,0,1:T(8,128)(2,1)S(1)}, bf16[256,2,128]{2,0,1:T(8,128)(2,1)}, u32[]{:S(2)}, u32[]{:S(2)}) collective-permute-start(bf16[256,2,128]{2,0,1:T(8,128)(2,1)S(1)} %get-tuple-element.213), channel_id=1, source_target_pairs={{4,0},{8,4},{12,8},{16,12},{20,16},{24,20},{28,24},{32,28},{36,32}... | collective-permute-start | bytes 393224 | tf_op jit(solution)/shard_map/ppermute | solution.py:17
  130.3 24.0 %collective-permute-start.15 = (bf16[256,2,128]{2,0,1:T(8,128)(2,1)S(1)}, bf16[256,2,128]{2,0,1:T(8,128)(2,1)}, u32[]{:S(2)}, u32[]{:S(2)}) collective-permute-start(bf16[256,2,128]{2,0,1:T(8,128)(2,1)S(1)} %get-tuple-element.220), channel_id=1, source_target_pairs={{16,0},{20,4},{24,8},{28,12},{32,16},{36,20},{40,24},{44,28},{48,3... | collective-permute-start | bytes 393224 | tf_op jit(solution)/shard_map/ppermute | solution.py:17
  131.2 15.3 %copy-start.35 = (bf16[256,2,128]{2,0,1:T(8,128)(2,1)}, bf16[256,2,128]{2,0,1:T(8,128)(2,1)S(1)}, u32[]{:S(2)}) copy-start(bf16[256,2,128]{2,0,1:T(8,128)(2,1)S(1)} %collective-permute-done.19) | copy-start | bytes 393220
  131.2 23.1 %collective-permute-start.14 = (bf16[256,2,128]{2,0,1:T(8,128)(2,1)S(1)}, bf16[256,2,128]{2,0,1:T(8,128)(2,1)}, u32[]{:S(2)}, u32[]{:S(2)}) collective-permute-start(bf16[256,2,128]{2,0,1:T(8,128)(2,1)S(1)} %get-tuple-element.218), channel_id=1, source_target_pairs={{12,0},{16,4},{20,8},{24,12},{28,16},{32,20},{36,24},{40,28},{44,3... | collective-permute-start | bytes 393224 | tf_op jit(solution)/shard_map/ppermute | solution.py:17
  140.9 5.5 %copy-start.37 = (bf16[256,2,128]{2,0,1:T(8,128)(2,1)}, bf16[256,2,128]{2,0,1:T(8,128)(2,1)S(1)}, u32[]{:S(2)}) copy-start(bf16[256,2,128]{2,0,1:T(8,128)(2,1)S(1)} %collective-permute-done.18) | copy-start | bytes 393220
  140.9 13.4 %collective-permute-start.13 = (bf16[256,2,128]{2,0,1:T(8,128)(2,1)S(1)}, bf16[256,2,128]{2,0,1:T(8,128)(2,1)}, u32[]{:S(2)}, u32[]{:S(2)}) collective-permute-start(bf16[256,2,128]{2,0,1:T(8,128)(2,1)S(1)} %get-tuple-element.219), channel_id=1, source_target_pairs={{8,0},{12,4},{16,8},{20,12},{24,16},{28,20},{32,24},{36,28},{40,32... | collective-permute-start | bytes 393224 | tf_op jit(solution)/shard_map/ppermute | solution.py:17
  143.9 11.7 %collective-permute-start.12 = (bf16[256,2,128]{2,0,1:T(8,128)(2,1)S(1)}, bf16[256,2,128]{2,0,1:T(8,128)(2,1)}, u32[]{:S(2)}, u32[]{:S(2)}) collective-permute-start(bf16[256,2,128]{2,0,1:T(8,128)(2,1)S(1)} %get-tuple-element.217), channel_id=1, source_target_pairs={{4,0},{8,4},{12,8},{16,12},{20,16},{24,20},{28,24},{32,28},{36,32}... | collective-permute-start | bytes 393224 | tf_op jit(solution)/shard_map/ppermute | solution.py:17
  147.9 5.6 %copy-start.18 = (f32[2,320,2,128]{3,1,2,0:T(8,128)S(1)}, f32[2,320,2,128]{3,1,2,0:T(8,128)}, u32[]{:S(2)}) copy-start(f32[2,320,2,128]{3,1,2,0:T(8,128)} %convolution_bitcast_fusion.7) | copy-start | bytes 1966084
  147.9 5.8 %copy-start.19 = (f32[2,320,2,128]{3,1,2,0:T(8,128)S(1)}, f32[2,320,2,128]{3,1,2,0:T(8,128)}, u32[]{:S(2)}) copy-start(f32[2,320,2,128]{3,1,2,0:T(8,128)} %convolution_bitcast_fusion.6) | copy-start | bytes 1966084
  147.9 7.7 %copy-start.28 = (f32[2,256,128]{2,1,0:T(8,128)S(1)}, f32[2,256,128]{2,1,0:T(8,128)}, u32[]{:S(2)}) copy-start(f32[2,256,128]{2,1,0:T(8,128)} %get-tuple-element.56) | copy-start | bytes 786436
  147.9 7.7 %copy-start.31 = (f32[2,256,128]{2,1,0:T(8,128)S(1)}, f32[2,256,128]{2,1,0:T(8,128)}, u32[]{:S(2)}) copy-start(f32[2,256,128]{2,1,0:T(8,128)} %get-tuple-element.57) | copy-start | bytes 786436
  147.9 7.7 %copy-start.36 = (bf16[256,2,128]{2,0,1:T(8,128)(2,1)S(1)}, bf16[256,2,128]{2,0,1:T(8,128)(2,1)}, u32[]{:S(2)}) copy-start(bf16[256,2,128]{2,0,1:T(8,128)(2,1)} %copy-done.35) | copy-start | bytes 393220
  148.0 7.7 %copy-start.38 = (bf16[256,2,128]{2,0,1:T(8,128)(2,1)S(1)}, bf16[256,2,128]{2,0,1:T(8,128)(2,1)}, u32[]{:S(2)}) copy-start(bf16[256,2,128]{2,0,1:T(8,128)(2,1)} %copy-done.37) | copy-start | bytes 393220
  148.0 7.7 %copy-start.40 = (bf16[256,2,128]{2,0,1:T(8,128)(2,1)S(1)}, bf16[256,2,128]{2,0,1:T(8,128)(2,1)}, u32[]{:S(2)}) copy-start(bf16[256,2,128]{2,0,1:T(8,128)(2,1)} %copy-done.39) | copy-start | bytes 393220
  153.8 3.6 %copy-start.17 = (bf16[384,256]{0,1:T(8,128)(2,1)S(1)}, bf16[384,256]{0,1:T(8,128)(2,1)}, u32[]{:S(2)}) copy-start(bf16[384,256]{0,1:T(8,128)(2,1)} %copy-done.16) | copy-start | bytes 589828
  153.8 3.6 %copy-start.44 = (f32[384,2]{0,1:T(2,128)S(1)}, f32[384,2]{0,1:T(2,128)}, u32[]{:S(2)}) copy-start(f32[384,2]{0,1:T(2,128)} %copy-done.43) | copy-start | bytes 9220
  153.8 3.6 %copy-start.46 = (f32[384,2]{0,1:T(2,128)S(1)}, f32[384,2]{0,1:T(2,128)}, u32[]{:S(2)}) copy-start(f32[384,2]{0,1:T(2,128)} %get-tuple-element.225) | copy-start | bytes 9220
  153.8 3.6 %copy-start.54 = (f32[256]{0:T(256)S(1)}, f32[256]{0:T(256)}, u32[]{:S(2)}) copy-start(f32[256]{0:T(256)} %broadcast_bitcast_fusion.1) | copy-start | bytes 3076
  (53 other events, 89.6 us)
where the time goes:
time: 242 us; the launch traced here: 238 us
  blocking collectives  78.2 us (32%)
  local copies, waits for them, and re-layouts  40.6 us (17%)
  starting transfers between devices  34.1 us (14%)
  other arithmetic  29.1 us (12%)
  waiting for transfers between devices  27.5 us (11%)
  matrix products  25.5 us (11%)
    psum x1, blocking collectives, on_device(): lax.psum((query_portion, key_portion), ('dp', 'tensor'))  78.2 us
    ppermute x20, starting transfers between devices, passed_along(): return lax.ppermute(block, axis, route)  34.1 us
    ppermute x20, waiting for transfers between devices, passed_along(): return lax.ppermute(block, axis, route)  27.5 us
    unnamed x93, local copies, waits for them, and re-layouts  11.2 us
    while x70, local copies, waits for them, and re-layouts  6.76 us
    sub x2, matrix products, attend(): raised = jnp.exp(scores - row_max)  6.41 us
    reduce_sum x4, other arithmetic, norm_backward(): jnp.sum((upstream * widened * inverse).reshape(-1, widened.shape[-1]), ax...  5.83 us
    dot_general x3, matrix products, attend(): jnp.einsum('gmn,mgd->nd', weights, d_rows, preferred_element_type=jnp.flo...  5.78 us
  transfers between devices with their start and end apart: 20, of which 8 were waited for; matrix products, arithmetic and copies ran while one was open for 25% of the time, Pallas kernels for 0%

commit v1 on v0

v1 whole, which is shorter than its diff:
```python
import functools

import jax
import jax.numpy as jnp
from jax import lax
from jax.experimental import pallas as pl
from jax.experimental.pallas import tpu as pltpu
from jax.sharding import PartitionSpec as P

PROMPT = 256
RESP = 64
HEAD = 128
KEYS = PROMPT + RESP
EPSILON = 1e-06
SCALE = HEAD ** (-0.5)
LOG2E = 1.4426950408889634
SHARP = SCALE * LOG2E
MASKED = -1e30
MESH = pl.DeviceIdType.MESH
F32 = jnp.float32
BF16 = jnp.bfloat16
NT = (((1,), (1,)), ((), ()))


def dot_nn(a, b):
    return jnp.dot(a, b, preferred_element_type=F32)


def dot_nt(a, b):
    return lax.dot_general(a, b, NT, preferred_element_type=F32)


def normed_rows(rows):
    wide = rows.astype(F32)
    inverse = lax.rsqrt(jnp.mean(wide * wide, axis=1, keepdims=True) + EPSILON)
    return wide, inverse


def softmax_columns(blocks, keep):
    top = functools.reduce(jnp.maximum, [jnp.max(b, axis=0, keepdims=True) for b in blocks])
    shift = top * SHARP
    raised = [jnp.exp2(b * SHARP - shift) for b in blocks]
    total = functools.reduce(jnp.add, [jnp.sum(b, axis=0, keepdims=True) for b in raised])
    factor = keep / total
    return [b * factor for b in raised]


def score_gradient(probs, weights, p_grads):
    inner = functools.reduce(
        jnp.add,
        [
            jnp.sum(w.astype(F32) * g, axis=0, keepdims=True)
            for w, g in zip(weights, p_grads, strict=True)
        ],
    )
    return [(p * (g - inner)).astype(BF16) for p, g in zip(probs, p_grads, strict=True)]


def kernel(
    heads,
    groups,
    n_dp,
    n_tensor,
    plen,
    rlen,
    rown,
    qg,
    kg,
    q_hbm,
    k_hbm,
    v_hbm,
    o_hbm,
    dq_hbm,
    dk_out,
    dv_out,
    qg_out,
    kg_out,
    qv,
    ov,
    dqv,
    kself,
    vself,
    near_k0,
    near_k1,
    near_v0,
    near_v1,
    eye,
    gain_col,
    bias_p,
    bias_own,
    kn_p,
    knt_p,
    dk_acc,
    dv_acc,
    qg_acc,
    kg_acc,
    r_o,
    r_qt,
    r_qnt,
    r_inv,
    r_k,
    r_kt,
    r_khat,
    r_p,
    r_v,
    r_dv,
    r_dk,
    back,
    back_sib,
    back_r4,
    back_r2,
    back_o4,
    back_o2,
    part_a,
    part_b,
    buf_a,
    buf_b,
    load_sem,
    store_sem,
    fwd_send,
    fwd_recv,
    bwd_send,
    bwd_recv,
    a_send,
    a_recv,
    b_send,
    b_recv,
):
    dp = lax.axis_index("dp")
    tensor = lax.axis_index("tensor")
    core = lax.rem(dp, 2)
    up = (lax.rem(dp + 2, n_dp), tensor)
    down = (lax.rem(dp + n_dp - 2, n_dp), tensor)
    sibling = (dp + 1 - 2 * core, tensor)
    near = (near_k0, near_k1, near_v0, near_v1)
    chunks = 2 * heads

    columns = n_dp // 16
    n_a = columns * n_tensor
    place_a = lax.div(dp, 16) * n_tensor + tensor
    place_b = lax.rem(dp, 16)

    def peer_a(k):
        place = lax.rem(place_a + k, n_a)
        return place, (lax.div(place, n_tensor) * 16 + place_b, lax.rem(place, n_tensor))

    def peer_b(k):
        place = lax.rem(place_b + k, 16)
        return place, (dp - place_b + place, tensor)

    def cols(h, g=None):
        if g is None:
            return pl.ds(h * HEAD, HEAD)
        return pl.ds(pl.multiple_of((h * groups + g) * HEAD, HEAD), HEAD)

    loads = []

    def load(src, dst):
        copy = pltpu.make_async_copy(src, dst, load_sem.at[len(loads)])
        copy.start()
        loads.append(copy)
        return copy

    staged = []
    for c in range(chunks):
        h = c % heads
        source = (k_hbm if c < heads else v_hbm).at[pl.ds(0, PROMPT), cols(h)]
        staged.append(load(source, near[c].at[0, pl.ds(0, PROMPT)]))
    load_k = load(k_hbm, kself)
    wide = groups * HEAD
    load_q, load_o = [], []
    for h in range(heads):
        load_q.append(load(q_hbm.at[:, pl.ds(h * wide, wide)], qv.at[:, pl.ds(h * wide, wide)]))
        load_o.append(load(o_hbm.at[:, pl.ds(h * wide, wide)], ov.at[:, pl.ds(h * wide, wide)]))
        if h == 0:
            load_v = load(v_hbm, vself)

    barrier = pltpu.get_barrier_semaphore()
    for neighbour in (up, down):
        pl.semaphore_signal(barrier, inc=1, device_id=neighbour, device_id_type=MESH)

    @pl.loop(1, 16)
    def _(k):
        pl.semaphore_signal(barrier, inc=1, device_id=peer_b(k)[1], device_id_type=MESH)

    if n_a > 1:

        @pl.loop(1, n_a)
        def _(k):
            pl.semaphore_signal(barrier, inc=1, device_id=peer_a(k)[1], device_id_type=MESH)

    row_at = lax.broadcasted_iota(jnp.int32, (HEAD, HEAD), 0)
    col_at = lax.broadcasted_iota(jnp.int32, (HEAD, HEAD), 1)
    eye[...] = jnp.where(row_at == col_at, 1.0, 0.0).astype(BF16)
    gain_col[...] = jnp.broadcast_to(qg[...], (HEAD, HEAD)).T
    length = plen[0]
    key_at = lax.broadcasted_iota(jnp.int32, (PROMPT, PROMPT), 0)
    query_at = lax.broadcasted_iota(jnp.int32, (PROMPT, PROMPT), 1)
    bias_p[...] = jnp.where((key_at <= query_at) & (key_at < length), 0.0, MASKED)
    own_key = lax.broadcasted_iota(jnp.int32, (RESP, HEAD), 0)
    own_query = lax.rem(lax.broadcasted_iota(jnp.int32, (RESP, HEAD), 1), RESP)
    bias_own[...] = jnp.where(own_key <= own_query, 0.0, MASKED)
    near_k0[0, pl.ds(PROMPT, 16)] = jnp.full((16, HEAD), length.astype(F32)).astype(BF16)
    qg_acc[...] = jnp.zeros_like(qg_acc)
    kg_acc[...] = jnp.zeros_like(kg_acc)
    dk_acc[...] = jnp.zeros_like(dk_acc)
    dv_acc[...] = jnp.zeros_like(dv_acc)
    keep_p = (lax.broadcasted_iota(jnp.int32, (1, PROMPT), 1) < length).astype(F32)
    picks = [lax.rem(dp + n_dp - rown[s], n_dp) for s in range(2)]

    for copy in staged:
        copy.wait()
    pl.semaphore_wait(barrier, 2 + 15 + n_a - 1)

    def slot(c, d):
        return near[c].at[d]

    def forward(kind, c, src, dst, device):
        return pltpu.make_async_remote_copy(
            src_ref=slot(c, src),
            dst_ref=slot(c, dst),
            send_sem=fwd_send.at[kind, c],
            recv_sem=fwd_recv.at[kind, c],
            device_id=device,
            device_id_type=MESH,
        )

    def hop(c):
        return forward(0, c, 0, 2, up)

    def relay(c):
        return forward(1, c, 2, 4, up)

    def across(c, far, src):
        return forward(2 + far, c, src, 1 + 2 * far, sibling)

    def send_own(c):
        hop(c).start()

        @pl.when(core == 0)
        def _():
            across(c, 0, 0).start()

    def pass_on(c):
        hop(c).wait_recv()
        relay(c).start()

        @pl.when(core == 0)
        def _():
            across(c, 1, 2).start()

        @pl.when(core == 1)
        def _():
            across(c, 0, 2).start()

    def arrive(c):
        relay(c).wait_recv()

        @pl.when(core == 1)
        def _():
            across(c, 1, 4).start()

        across(c, 0, 0).wait_recv()
        across(c, 1, 0).wait_recv()

    def prepared(rows):
        qt = dot_nt(eye[...], rows)
        inverse = lax.rsqrt(jnp.mean(qt * qt, axis=0, keepdims=True) + EPSILON)
        gain = jnp.concatenate([gain_col[...]] * (qt.shape[1] // HEAD), axis=1)
        return qt, inverse, (qt * inverse * gain).astype(BF16)

    def query_backward(grad, qt, inverse):
        gain = jnp.concatenate([gain_col[...]] * (qt.shape[1] // HEAD), axis=1)
        both = grad * qt
        mean = jnp.mean(both * gain, axis=0, keepdims=True)
        scaled = inverse * SCALE
        out = grad * gain * scaled - qt * (inverse * inverse * scaled * mean)
        portion = both * scaled
        for at in range(0, qt.shape[1], HEAD):
            qg_acc[...] += portion[:, at : at + HEAD]
        return out.T.astype(BF16)

    def prepare_prompt_keys(h):
        wide_k, inverse = normed_rows(kself[pl.ds(0, PROMPT), cols(h)])
        normed = (wide_k * inverse * kg[...]).astype(BF16)
        kn_p[h] = normed
        knt_p[h] = dot_nt(eye[...], normed).astype(BF16)

    def prompt_unit(h, g):
        at = cols(h, g)
        qt, inverse, qnt = prepared(qv[pl.ds(0, PROMPT), at])
        rows_o = ov[pl.ds(0, PROMPT), at]
        scores = dot_nn(kn_p[h], qnt)
        p_grad = dot_nt(vself[pl.ds(0, PROMPT), cols(h)], rows_o)
        half = PROMPT // 2
        left = [scores[:half, :half] + bias_p[:half, :half]]
        right = [
            scores[:half, half:] + bias_p[:half, half:],
            scores[half:, half:] + bias_p[half:, half:],
        ]
        left_p = softmax_columns(left, keep_p[:, :half])
        right_p = softmax_columns(right, keep_p[:, half:])
        left_w = [p.astype(BF16) for p in left_p]
        right_w = [p.astype(BF16) for p in right_p]
        left_s = score_gradient(left_p, left_w, [p_grad[:half, :half]])
        right_s = score_gradient(right_p, right_w, [p_grad[:half, half:], p_grad[half:, half:]])
        empty = jnp.zeros((half, half), BF16)

        def square(a, b):
            return jnp.concatenate(
                [jnp.concatenate([a[0], empty], axis=0), jnp.concatenate(b, axis=0)], axis=1
            )

        weights = square(left_w, right_w)
        s_grad = square(left_s, right_s)
        dv_acc[h] += dot_nn(weights, rows_o)
        dk_acc[h] += dot_nt(s_grad, qnt)
        grad = dot_nn(knt_p[h], s_grad)
        dqv[pl.ds(0, PROMPT), at] = query_backward(grad, qt, inverse)

    def prompt_units(h, first, last):
        @pl.loop(first, last)
        def _(g):
            prompt_unit(h, g)

    def response_rows(s):
        return pl.ds(pl.multiple_of(PROMPT + s * RESP, RESP), RESP)

    def prepare_responses(h):
        @pl.loop(0, 2)
        def _(s):
            rows = response_rows(s)
            stacked = jnp.concatenate([qv[rows, cols(h, g)] for g in range(groups)], axis=0)
            r_o[h, s] = jnp.concatenate([ov[rows, cols(h, g)] for g in range(groups)], axis=0)
            qt, inverse, qnt = prepared(stacked)
            r_qt[h, s] = qt
            r_qnt[h, s] = qnt
            r_inv[h, s] = jnp.broadcast_to(inverse, (8, inverse.shape[1]))

    span = 2 * HEAD

    def response_keys(h):
        @pl.loop(0, 2)
        def _(s):
            pick = jnp.clip(lax.rem(dp + n_dp - rown[s], n_dp), 1, 4)
            rows = response_rows(s)
            wide_k, inverse = normed_rows(near[h][pick, pl.ds(0, PROMPT)])
            hat = wide_k * inverse
            r_khat[h, s, pl.ds(0, PROMPT)] = hat
            r_k[h, s, pl.ds(0, PROMPT)] = (hat * kg[...]).astype(BF16)
            wide_k, inverse = normed_rows(kself[rows, cols(h)])
            hat = wide_k * inverse
            r_khat[h, s, pl.ds(PROMPT, RESP)] = hat
            r_k[h, s, pl.ds(PROMPT, RESP)] = (hat * kg[...]).astype(BF16)
            normed = r_k[h, s]
            r_kt[h, s] = dot_nt(eye[...], normed).astype(BF16)
            owner_length = near_k0[pick, pl.ds(PROMPT, 16)].astype(F32)[0:1]
            at = lax.broadcasted_iota(jnp.int32, (PROMPT, HEAD), 0).astype(F32)
            bias = jnp.where(at < owner_length, 0.0, MASKED)
            bias = jnp.concatenate([bias, bias_own[...]], axis=0)
            bias = jnp.concatenate([bias, bias], axis=1)
            place = lax.rem(lax.broadcasted_iota(jnp.int32, (1, span), 1), RESP)
            keep = (place < rlen[s]).astype(F32)
            total = jnp.zeros((KEYS, HEAD), F32)
            for first in range(0, groups * RESP, span):
                block = pl.ds(first, span)
                scores = dot_nn(normed, r_qnt[h, s, :, block]) + bias
                (probs,) = softmax_columns([scores], keep)
                r_p[h, s, :, block] = probs
                total = total + dot_nn(probs.astype(BF16), r_o[h, s, block])
            r_dv[h, s] = total

    def response_values(h):
        @pl.loop(0, 2)
        def _(s):
            pick = jnp.clip(lax.rem(dp + n_dp - rown[s], n_dp), 1, 4)
            rows = response_rows(s)
            r_v[pl.ds(0, PROMPT)] = near[heads + h][pick]
            r_v[pl.ds(PROMPT, RESP)] = vself[rows, cols(h)]
            total = jnp.zeros((KEYS, HEAD), F32)
            for first in range(0, groups * RESP, span):
                block = pl.ds(first, span)
                probs = r_p[h, s, :, block]
                p_grad = dot_nt(r_v[...], r_o[h, s, block])
                (s_grad,) = score_gradient([probs], [probs.astype(BF16)], [p_grad])
                total = total + dot_nt(s_grad, r_qnt[h, s, :, block])
                grad = dot_nn(r_kt[h, s], s_grad)
                out = query_backward(grad, r_qt[h, s, :, block], r_inv[h, s, 0:1, block])
                for i in range(span // RESP):
                    dqv[rows, cols(h, first // RESP + i)] = out[i * RESP : (i + 1) * RESP]
            r_dk[h, s] = total
            portion = total * r_khat[h, s] * SCALE
            kg_acc[...] += jnp.sum(portion.reshape(KEYS // 8, 8, HEAD), axis=0)

    def key_backward(grad, rows):
        wide_k, inverse = normed_rows(rows)
        scaled = grad * kg[...]
        mean = jnp.mean(scaled * wide_k, axis=1, keepdims=True)
        factor = inverse * SCALE
        return (scaled * factor - wide_k * (inverse * inverse * factor * mean)).astype(BF16)

    def backward(kind, c, src, dst, device):
        return pltpu.make_async_remote_copy(
            src_ref=src,
            dst_ref=dst,
            send_sem=bwd_send.at[kind, c],
            recv_sem=bwd_recv.at[kind, c],
            device_id=device,
            device_id_type=MESH,
        )

    def back_across(c):
        return backward(0, c, back.at[c, pl.ds(0, 2)], back_sib.at[c], sibling)

    def back_far(c):
        return backward(1, c, back_o4.at[c], back_r4.at[c], down)

    def back_near(c):
        return backward(2, c, back_o2.at[c], back_r2.at[c], down)

    def give_back(c, terms):
        for i, distance in enumerate((1, 3, 2, 4)):
            first = (picks[0] == distance).astype(F32)
            second = (picks[1] == distance).astype(F32)
            term = first * terms[0, pl.ds(0, PROMPT)] + second * terms[1, pl.ds(0, PROMPT)]
            back[c, i] = term.astype(BF16)
        back_across(c).start()

    upper = core.astype(F32)

    def give_back_far(c):
        back_across(c).wait_recv()
        total = back[c, 3].astype(F32) + upper * back_sib[c, 1].astype(F32)
        back_o4[c] = total.astype(BF16)
        back_far(c).start()

    def give_back_near(c):
        back_far(c).wait_recv()
        other = upper * back_sib[c, 0].astype(F32) + (1.0 - upper) * back_sib[c, 1].astype(F32)
        total = back[c, 2].astype(F32) + back_r4[c].astype(F32) + other
        back_o2[c] = total.astype(BF16)
        back_near(c).start()

    def taken_back(c):
        back_near(c).wait_recv()
        return back_r2[c].astype(F32) + (1.0 - upper) * back_sib[c, 0].astype(F32)

    def exchange(n, peer, place, source, buffer, send_sem, recv_sem):
        def copy(k):
            other, device = peer(k)
            return pltpu.make_async_remote_copy(
                src_ref=source,
                dst_ref=buffer.at[place],
                send_sem=send_sem.at[other],
                recv_sem=recv_sem.at[place],
                device_id=device,
                device_id_type=MESH,
            )

        def arriving(k):
            other, device = peer(k)
            return pltpu.make_async_remote_copy(
                src_ref=source,
                dst_ref=buffer.at[other],
                send_sem=send_sem.at[other],
                recv_sem=recv_sem.at[other],
                device_id=device,
                device_id_type=MESH,
            )

        def start():
            if n > 1:

                @pl.loop(1, n)
                def _(k):
                    copy(k).start()

        def collect():
            buffer[place] = source[...]
            if n > 1:

                @pl.loop(1, n)
                def _(k):
                    arriving(k).wait_recv()

            total = buffer[0]
            for i in range(1, n):
                total = total + buffer[i]
            return total

        def finish():
            if n > 1:

                @pl.loop(1, n)
                def _(k):
                    copy(k).wait_send()

        return start, collect, finish

    start_a, collect_a, finish_a = exchange(n_a, peer_a, place_a, part_a, buf_a, a_send, a_recv)
    start_b, collect_b, finish_b = exchange(16, peer_b, place_b, part_b, buf_b, b_send, b_recv)

    for c in range(chunks):
        send_own(c)
    load_k.wait()
    load_v.wait()
    load_q[0].wait()
    load_o[0].wait()
    prepare_prompt_keys(0)
    prompt_units(0, 0, groups)
    load_q[1].wait()
    load_o[1].wait()
    prepare_prompt_keys(1)
    pass_on(0)
    prepare_responses(0)
    prepare_responses(1)
    pass_on(1)
    prompt_units(1, 0, 3)
    pass_on(2)
    prompt_units(1, 3, 6)
    pass_on(3)
    prompt_units(1, 6, groups)
    stores = [
        pltpu.make_async_copy(
            dqv.at[pl.ds(0, PROMPT)], dq_hbm.at[pl.ds(0, PROMPT)], store_sem.at[0]
        )
    ]
    stores[0].start()
    for h in range(heads):
        portion = jnp.zeros((8, HEAD), F32)
        wide_k, inverse = normed_rows(kself[pl.ds(0, PROMPT), cols(h)])
        portion = dk_acc[h] * (wide_k * inverse) * SCALE
        kg_acc[...] += jnp.sum(portion.reshape(PROMPT // 8, 8, HEAD), axis=0)

    arrive(0)
    response_keys(0)
    give_back(2, r_dv.at[0])
    arrive(1)
    response_keys(1)
    give_back(3, r_dv.at[1])
    give_back_far(2)
    arrive(2)
    response_values(0)
    give_back(0, r_dk.at[0])
    give_back_far(3)
    arrive(3)
    response_values(1)
    give_back(1, r_dk.at[1])
    part_a[...] = jnp.concatenate(
        [
            jnp.sum(qg_acc[...].T, axis=0, keepdims=True),
            jnp.sum(kg_acc[...], axis=0, keepdims=True),
            jnp.zeros((6, HEAD), F32),
        ],
        axis=0,
    )
    start_a()
    give_back_far(0)
    give_back_far(1)
    stores.append(
        pltpu.make_async_copy(
            dqv.at[pl.ds(PROMPT, 2 * RESP)], dq_hbm.at[pl.ds(PROMPT, 2 * RESP)], store_sem.at[1]
        )
    )
    stores[1].start()
    give_back_near(2)
    give_back_near(3)
    give_back_near(0)
    for h in range(heads):
        for s in range(2):
            rows = pl.ds(PROMPT + s * RESP, RESP)
            dv_out[rows, cols(h)] = r_dv[h, s, pl.ds(PROMPT, RESP)].astype(BF16)
            dk_out[rows, cols(h)] = key_backward(
                r_dk[h, s, pl.ds(PROMPT, RESP)], kself[rows, cols(h)]
            )
    part_b[...] = collect_a()
    start_b()
    give_back_near(1)
    prompt = pl.ds(0, PROMPT)
    for h in range(heads):
        dv_out[prompt, cols(h)] = (dv_acc[h] + taken_back(heads + h)).astype(BF16)
    for h in range(heads):
        dk_out[prompt, cols(h)] = key_backward(
            dk_acc[h] + taken_back(h), kself[prompt, cols(h)]
        )
    sums = collect_b()
    qg_out[...] = sums[0:1]
    kg_out[...] = sums[1:2]

    finish_a()
    finish_b()
    for c in range(chunks):
        hop(c).wait_send()
        relay(c).wait_send()
        across(c, 0, 0).wait_send()
        across(c, 1, 0).wait_send()
        back_across(c).wait_send()
        back_far(c).wait_send()
        back_near(c).wait_send()
    for copy in stores:
        copy.wait()


def on_device(
    n_dp, n_tensor, queries, keys, values, output_gradient, q_gain, k_gain, prompt_len, resp_len, resp_owner
):
    heads = keys.shape[1] // HEAD
    groups = queries.shape[1] // keys.shape[1]
    rows = queries.shape[0]
    chunks = 2 * heads
    n_a = n_dp // 16 * n_tensor
    vmem = pl.BlockSpec(memory_space=pltpu.VMEM)
    smem = pl.BlockSpec(memory_space=pltpu.SMEM)
    hbm = pl.BlockSpec(memory_space=pltpu.HBM)
    asked = groups * RESP
    scratch = [
        pltpu.VMEM(queries.shape, BF16),
        pltpu.VMEM(queries.shape, BF16),
        pltpu.VMEM(queries.shape, BF16),
        pltpu.VMEM(keys.shape, BF16),
        pltpu.VMEM(keys.shape, BF16),
        pltpu.VMEM((5, PROMPT + 16, HEAD), BF16),
        pltpu.VMEM((5, PROMPT, HEAD), BF16),
        pltpu.VMEM((5, PROMPT, HEAD), BF16),
        pltpu.VMEM((5, PROMPT, HEAD), BF16),
        pltpu.VMEM((HEAD, HEAD), BF16),
        pltpu.VMEM((HEAD, HEAD), F32),
        pltpu.VMEM((PROMPT, PROMPT), F32),
        pltpu.VMEM((RESP, HEAD), F32),
        pltpu.VMEM((heads, PROMPT, HEAD), BF16),
        pltpu.VMEM((heads, HEAD, PROMPT), BF16),
        pltpu.VMEM((heads, PROMPT, HEAD), F32),
        pltpu.VMEM((heads, PROMPT, HEAD), F32),
        pltpu.VMEM((HEAD, HEAD), F32),
        pltpu.VMEM((8, HEAD), F32),
        pltpu.VMEM((heads, 2, asked, HEAD), BF16),
        pltpu.VMEM((heads, 2, HEAD, asked), F32),
        pltpu.VMEM((heads, 2, HEAD, asked), BF16),
        pltpu.VMEM((heads, 2, 8, asked), F32),
        pltpu.VMEM((heads, 2, KEYS, HEAD), BF16),
        pltpu.VMEM((heads, 2, HEAD, KEYS), BF16),
        pltpu.VMEM((heads, 2, KEYS, HEAD), F32),
        pltpu.VMEM((heads, 2, KEYS, asked), F32),
        pltpu.VMEM((KEYS, HEAD), BF16),
        pltpu.VMEM((heads, 2, KEYS, HEAD), F32),
        pltpu.VMEM((heads, 2, KEYS, HEAD), F32),
        pltpu.VMEM((chunks, 4, PROMPT, HEAD), BF16),
        pltpu.VMEM((chunks, 2, PROMPT, HEAD), BF16),
        pltpu.VMEM((chunks, PROMPT, HEAD), BF16),
        pltpu.VMEM((chunks, PROMPT, HEAD), BF16),
        pltpu.VMEM((chunks, PROMPT, HEAD), BF16),
        pltpu.VMEM((chunks, PROMPT, HEAD), BF16),
        pltpu.VMEM((8, HEAD), F32),
        pltpu.VMEM((8, HEAD), F32),
        pltpu.VMEM((n_a, 8, HEAD), F32),
        pltpu.VMEM((16, 8, HEAD), F32),
        pltpu.SemaphoreType.DMA((chunks + 2 + 2 * heads,)),
        pltpu.SemaphoreType.DMA((2,)),
        pltpu.SemaphoreType.DMA((4, chunks)),
        pltpu.SemaphoreType.DMA((4, chunks)),
        pltpu.SemaphoreType.DMA((3, chunks)),
        pltpu.SemaphoreType.DMA((3, chunks)),
        pltpu.SemaphoreType.DMA((n_a,)),
        pltpu.SemaphoreType.DMA((n_a,)),
        pltpu.SemaphoreType.DMA((16,)),
        pltpu.SemaphoreType.DMA((16,)),
    ]
    q_grad, k_grad, v_grad, q_gain_grad, k_gain_grad = pl.pallas_call(
        functools.partial(kernel, heads, groups, n_dp, n_tensor),
        out_shape=(
            jax.ShapeDtypeStruct(queries.shape, BF16),
            jax.ShapeDtypeStruct(keys.shape, BF16),
            jax.ShapeDtypeStruct(keys.shape, BF16),
            jax.ShapeDtypeStruct((1, HEAD), F32),
            jax.ShapeDtypeStruct((1, HEAD), F32),
        ),
        in_specs=[smem, smem, smem, vmem, vmem, hbm, hbm, hbm, hbm],
        out_specs=(hbm, vmem, vmem, vmem, vmem),
        scratch_shapes=scratch,
        compiler_params=pltpu.CompilerParams(
            collective_id=0, has_side_effects=True, vmem_limit_bytes=56 * 2**20
        ),
        name="attention",
    )(
        prompt_len,
        resp_len,
        resp_owner,
        q_gain.reshape(1, HEAD),
        k_gain.reshape(1, HEAD),
        queries,
        keys,
        values,
        output_gradient,
    )
    return q_grad, k_grad, v_grad, q_gain_grad.reshape(HEAD), k_gain_grad.reshape(HEAD)


def solution(mesh):
    rows, whole = P("dp", "tensor"), P()
    return jax.shard_map(
        functools.partial(on_device, mesh.shape["dp"], mesh.shape["tensor"]),
        mesh=mesh,
        in_specs=(rows, rows, rows, rows, whole, whole, P("dp"), P("dp"), P("dp")),
        out_specs=(rows, rows, rows, whole, whole),
        check_vma=False,
    )
```

time: 242 us -> 56.1 us (0.23); the launches traced: 238 us -> 56 us
  blocking collectives: 78.2 us -> 0 us
  Pallas kernels: 0 us -> 49.5 us
  local copies, waits for them, and re-layouts: 40.6 us -> 5.18 us
  starting transfers between devices: 34.1 us -> 0 us
  other arithmetic: 29.1 us -> 0 us
  waiting for transfers between devices: 27.5 us -> 0 us
  matrix products: 25.5 us -> 0 us
    psum x1 -> x0, blocking collectives: 78.2 us -> none  [on_device(): lax.psum((query_portion, key_portion), ('dp', 'tensor'))]
    pallas_call x0 -> x1, Pallas kernels: none -> 49.5 us  [on_device(): pl.pallas_call(functools.partial(kernel, heads, groups, n_dp, n_tensor),...]
    ppermute x20 -> x0, starting transfers between devices: 34.1 us -> none  [passed_along(): return lax.ppermute(block, axis, route)]
    ppermute x20 -> x0, waiting for transfers between devices: 27.5 us -> none  [passed_along(): return lax.ppermute(block, axis, route)]
    dot_general x16 -> x0, matrix products: 19.1 us -> none  [the longest x3 5.78 us: attend(): jnp.einsum('gmn,mgd->nd', weights, d_rows, preferred_element_type=jnp.flo...]
    reduce_sum x10 -> x0, other arithmetic: 11.7 us -> none  [the longest x4 5.83 us: norm_backward(): jnp.sum((upstream * widened * inverse).reshape(-1, widened.shape[-1]), ax...]
    while x70 -> x0, local copies, waits for them, and re-layouts: 6.76 us -> none
    sub x2 -> x0, matrix products: 6.41 us -> none  [attend(): raised = jnp.exp(scores - row_max)]
  transfers between devices with their start and end apart: 20 -> 0, of which waited for: 8 -> 0; matrix products, arithmetic and copies ran while one was open for 25% -> 0% of each run, Pallas kernels for 0% -> 0%
where the time goes in v1:
time: 56.1 us; the launch traced here: 56 us
  Pallas kernels  49.5 us (88%)
  local copies, waits for them, and re-layouts  5.18 us (9%)
  between operations  1.32 us (2%)
    pallas_call x1, Pallas kernels, on_device(): pl.pallas_call(functools.partial(kernel, heads, groups, n_dp, n_tensor),...  49.5 us
    unnamed x13, local copies, waits for them, and re-layouts  5.18 us

profile of v1, /device:TPU:1, one launch (start us, length us, event | category | flops | bytes accessed | tf_op | source)
XLA Modules:
  0.0 56.0 jit_solution(17290115098703568563)
XLA Ops:
  1.3 49.5 %attention.1 = (bf16[384,2048]{1,0:T(8,128)(2,1)}, bf16[384,256]{1,0:T(8,128)(2,1)}, bf16[384,256]{1,0:T(8,128)(2,1)}, f32[1,128]{1,0:T(1,128)}, f32[1,128]{1,0:T(1,128)}) custom-call(s32[1]{0:T(128)S(6)} %copy.19.plen, s32[2]{0:T(128)} %rlen.1, s32[2]{0:T(128)} %rown.1, f32[1,128]{1,0:T(1,128)} %bitcast.4, f32[1,128]{1,0:T(1,128)} %bitcast.5, ...), custom_call_target="tpu_custom_call" | custom-call | tf_op jit(solution)/shard_map/attention/pallas_call | solution.py:668
  50.8 0.0 copy-start.1
  50.8 0.0 copy-start
  50.8 0.0 copy-start.3
  50.8 0.0 copy-start.2
  50.8 2.8 %copy.20 = bf16[384,2048]{1,0:T(8,128)(2,1)} copy(bf16[384,2048]{1,0:T(8,128)(2,1)} %get-tuple-element.20) | data formatting | bytes 3145728
  53.6 0.0 copy-done.1
  53.6 0.7 %copy.21 = bf16[384,256]{1,0:T(8,128)(2,1)} copy(bf16[384,256]{1,0:T(8,128)(2,1)S(1)} %copy-done.1) | data formatting | bytes 393216
  54.3 0.0 copy-done
  54.3 0.7 %copy.22 = bf16[384,256]{1,0:T(8,128)(2,1)} copy(bf16[384,256]{1,0:T(8,128)(2,1)S(1)} %copy-done) | data formatting | bytes 393216
  55.0 0.0 copy-done.3
  55.0 0.5 copy.23
  55.5 0.0 copy-done.2
  55.5 0.5 copy.24
Async XLA Ops:
  50.8 2.8 %copy-start.1 = (bf16[384,256]{1,0:T(8,128)(2,1)S(1)}, bf16[384,256]{1,0:T(8,128)(2,1)}, u32[]{:S(2)}) copy-start(bf16[384,256]{1,0:T(8,128)(2,1)} %get-tuple-element.21) | copy-start | bytes 589828
  50.8 3.5 %copy-start = (bf16[384,256]{1,0:T(8,128)(2,1)S(1)}, bf16[384,256]{1,0:T(8,128)(2,1)}, u32[]{:S(2)}) copy-start(bf16[384,256]{1,0:T(8,128)(2,1)} %get-tuple-element.22) | copy-start | bytes 589828
  50.8 4.2 %copy-start.3 = (f32[1,128]{1,0:T(1,128)S(1)}, f32[1,128]{1,0:T(1,128)}, u32[]{:S(2)}) copy-start(f32[1,128]{1,0:T(1,128)} %get-tuple-element.13) | copy-start | bytes 1540
  50.8 4.7 %copy-start.2 = (f32[1,128]{1,0:T(1,128)S(1)}, f32[1,128]{1,0:T(1,128)}, u32[]{:S(2)}) copy-start(f32[1,128]{1,0:T(1,128)} %get-tuple-element.14) | copy-start | bytes 1540

commit v2 on v1

--- a/solution.py
+++ b/solution.py
@@ -70,14 +70,12 @@
     k_hbm,
     v_hbm,
     o_hbm,
-    dq_hbm,
+    dqv,
     dk_out,
     dv_out,
-    qg_out,
-    kg_out,
+    gains_out,
     qv,
     ov,
-    dqv,
     kself,
     vself,
     near_k0,
@@ -86,7 +84,8 @@
     near_v1,
     eye,
     gain_col,
-    bias_p,
+    bias_lower,
+    bias_upper,
     bias_own,
     kn_p,
     knt_p,
@@ -102,9 +101,6 @@
     r_kt,
     r_khat,
     r_p,
-    r_v,
-    r_dv,
-    r_dk,
     back,
     back_sib,
     back_r4,
@@ -116,7 +112,6 @@
     buf_a,
     buf_b,
     load_sem,
-    store_sem,
     fwd_send,
     fwd_recv,
     bwd_send,
@@ -189,24 +184,31 @@
         def _(k):
             pl.semaphore_signal(barrier, inc=1, device_id=peer_a(k)[1], device_id_type=MESH)
 
-    row_at = lax.broadcasted_iota(jnp.int32, (HEAD, HEAD), 0)
-    col_at = lax.broadcasted_iota(jnp.int32, (HEAD, HEAD), 1)
-    eye[...] = jnp.where(row_at == col_at, 1.0, 0.0).astype(BF16)
-    gain_col[...] = jnp.broadcast_to(qg[...], (HEAD, HEAD)).T
     length = plen[0]
-    key_at = lax.broadcasted_iota(jnp.int32, (PROMPT, PROMPT), 0)
-    query_at = lax.broadcasted_iota(jnp.int32, (PROMPT, PROMPT), 1)
-    bias_p[...] = jnp.where((key_at <= query_at) & (key_at < length), 0.0, MASKED)
-    own_key = lax.broadcasted_iota(jnp.int32, (RESP, HEAD), 0)
-    own_query = lax.rem(lax.broadcasted_iota(jnp.int32, (RESP, HEAD), 1), RESP)
-    bias_own[...] = jnp.where(own_key <= own_query, 0.0, MASKED)
+    query_at = lax.rem(lax.broadcasted_iota(jnp.int32, (1, PROMPT), 1), PROMPT // 2)
+    keep_lower = (query_at < length).astype(F32)
+    keep_upper = (query_at + PROMPT // 2 < length).astype(F32)
     near_k0[0, pl.ds(PROMPT, 16)] = jnp.full((16, HEAD), length.astype(F32)).astype(BF16)
-    qg_acc[...] = jnp.zeros_like(qg_acc)
-    kg_acc[...] = jnp.zeros_like(kg_acc)
-    dk_acc[...] = jnp.zeros_like(dk_acc)
-    dv_acc[...] = jnp.zeros_like(dv_acc)
-    keep_p = (lax.broadcasted_iota(jnp.int32, (1, PROMPT), 1) < length).astype(F32)
-    picks = [lax.rem(dp + n_dp - rown[s], n_dp) for s in range(2)]
+
+    def prepare():
+        row_at = lax.broadcasted_iota(jnp.int32, (HEAD, HEAD), 0)
+        col_at = lax.broadcasted_iota(jnp.int32, (HEAD, HEAD), 1)
+        eye[...] = jnp.where(row_at == col_at, 1.0, 0.0).astype(BF16)
+        gain_col[...] = jnp.broadcast_to(qg[...], (HEAD, HEAD)).T
+        for lower, bias in ((True, bias_lower), (False, bias_upper)):
+            key_at = lax.broadcasted_iota(jnp.int32, bias.shape, 0)
+            query_at = lax.rem(lax.broadcasted_iota(jnp.int32, bias.shape, 1), PROMPT // 2)
+            query_at = query_at if lower else query_at + PROMPT // 2
+            bias[...] = jnp.where((key_at <= query_at) & (key_at < length), 0.0, MASKED)
+        own_key = lax.broadcasted_iota(jnp.int32, (RESP, HEAD), 0)
+        own_query = lax.rem(lax.broadcasted_iota(jnp.int32, (RESP, HEAD), 1), RESP)
+        bias_own[...] = jnp.where(own_key <= own_query, 0.0, MASKED)
+        qg_acc[...] = jnp.zeros_like(qg_acc)
+        kg_acc[...] = jnp.zeros_like(kg_acc)
+        dk_acc[...] = jnp.zeros_like(dk_acc)
+        dv_acc[...] = jnp.zeros_like(dv_acc)
+
+    picks = [jnp.clip(lax.rem(dp + n_dp - rown[s], n_dp), 1, 4) for s in range(2)]
 
     for copy in staged:
         copy.wait()
@@ -276,9 +278,8 @@
         scaled = inverse * SCALE
         out = grad * gain * scaled - qt * (inverse * inverse * scaled * mean)
         portion = both * scaled
-        for at in range(0, qt.shape[1], HEAD):
-            qg_acc[...] += portion[:, at : at + HEAD]
-        return out.T.astype(BF16)
+        portion = sum(portion[:, at : at + HEAD] for at in range(0, qt.shape[1], HEAD))
+        return out.T.astype(BF16), portion
 
     def prepare_prompt_keys(h):
         wide_k, inverse = normed_rows(kself[pl.ds(0, PROMPT), cols(h)])
@@ -286,111 +287,113 @@
         kn_p[h] = normed
         knt_p[h] = dot_nt(eye[...], normed).astype(BF16)
 
-    def prompt_unit(h, g):
-        at = cols(h, g)
-        qt, inverse, qnt = prepared(qv[pl.ds(0, PROMPT), at])
-        rows_o = ov[pl.ds(0, PROMPT), at]
-        scores = dot_nn(kn_p[h], qnt)
-        p_grad = dot_nt(vself[pl.ds(0, PROMPT), cols(h)], rows_o)
-        half = PROMPT // 2
-        left = [scores[:half, :half] + bias_p[:half, :half]]
-        right = [
-            scores[:half, half:] + bias_p[:half, half:],
-            scores[half:, half:] + bias_p[half:, half:],
-        ]
-        left_p = softmax_columns(left, keep_p[:, :half])
-        right_p = softmax_columns(right, keep_p[:, half:])
-        left_w = [p.astype(BF16) for p in left_p]
-        right_w = [p.astype(BF16) for p in right_p]
-        left_s = score_gradient(left_p, left_w, [p_grad[:half, :half]])
-        right_s = score_gradient(right_p, right_w, [p_grad[:half, half:], p_grad[half:, half:]])
-        empty = jnp.zeros((half, half), BF16)
-
-        def square(a, b):
-            return jnp.concatenate(
-                [jnp.concatenate([a[0], empty], axis=0), jnp.concatenate(b, axis=0)], axis=1
-            )
-
-        weights = square(left_w, right_w)
-        s_grad = square(left_s, right_s)
-        dv_acc[h] += dot_nn(weights, rows_o)
-        dk_acc[h] += dot_nt(s_grad, qnt)
-        grad = dot_nn(knt_p[h], s_grad)
-        dqv[pl.ds(0, PROMPT), at] = query_backward(grad, qt, inverse)
-
-    def prompt_units(h, first, last):
-        @pl.loop(first, last)
-        def _(g):
-            prompt_unit(h, g)
+    half = PROMPT // 2
+
+    def prompt_head(h):
+        lo, hi = pl.ds(0, half), pl.ds(half, half)
+        parts = []
+        for pair in range(groups // 2):
+            at = [cols(h, 2 * pair + i) for i in range(2)]
+            parts.append((at, lo, lo, bias_lower, keep_lower))
+            parts.append((at, hi, pl.ds(0, PROMPT), bias_upper, keep_upper))
+        stacked = [jnp.concatenate([qv[r, a] for a in at], axis=0) for at, r, *_ in parts]
+        ready = [prepared(x) for x in stacked]
+        rows_o = [jnp.concatenate([ov[r, a] for a in at], axis=0) for at, r, *_ in parts]
+        p_grad = [dot_nt(vself[p[2], cols(h)], x) for p, x in zip(parts, rows_o)]
+        scores = [dot_nn(kn_p[h, p[2]], r[2]) + p[3][...] for p, r in zip(parts, ready)]
+        probs = [softmax_columns([x], p[4])[0] for p, x in zip(parts, scores)]
+        weights = [p.astype(BF16) for p in probs]
+        s_grad = [score_gradient([p], [w], [g])[0] for p, w, g in zip(probs, weights, p_grad)]
+        grad = [dot_nn(knt_p[h, :, p[2]], x) for p, x in zip(parts, s_grad)]
+        dv = [dot_nn(w, x) for w, x in zip(weights, rows_o)]
+        dk = [dot_nt(x, r[2]) for x, r in zip(s_grad, ready)]
+        for total, terms in ((dv_acc, dv), (dk_acc, dk)):
+            total[h, lo] += sum(terms[0::2]) + sum(t[:half] for t in terms[1::2])
+            total[h, hi] += sum(t[half:] for t in terms[1::2])
+        portions = []
+        for p, x, g in zip(parts, ready, grad):
+            out, portion = query_backward(g, x[0], x[1])
+            portions.append(portion)
+            for i, a in enumerate(p[0]):
+                dqv[p[1], a] = out[i * half : (i + 1) * half]
+        qg_acc[...] += sum(portions)
 
     def response_rows(s):
-        return pl.ds(pl.multiple_of(PROMPT + s * RESP, RESP), RESP)
+        return pl.ds(PROMPT + s * RESP, RESP)
 
     def prepare_responses(h):
-        @pl.loop(0, 2)
-        def _(s):
+        ready = []
+        for s in range(2):
             rows = response_rows(s)
             stacked = jnp.concatenate([qv[rows, cols(h, g)] for g in range(groups)], axis=0)
             r_o[h, s] = jnp.concatenate([ov[rows, cols(h, g)] for g in range(groups)], axis=0)
-            qt, inverse, qnt = prepared(stacked)
+            ready.append(prepared(stacked))
+        for s, (qt, inverse, qnt) in enumerate(ready):
             r_qt[h, s] = qt
             r_qnt[h, s] = qnt
             r_inv[h, s] = jnp.broadcast_to(inverse, (8, inverse.shape[1]))
+            wide_k, inverse = normed_rows(kself[response_rows(s), cols(h)])
+            hat = wide_k * inverse
+            r_khat[h, s, pl.ds(PROMPT, RESP)] = hat
+            r_k[h, s, pl.ds(PROMPT, RESP)] = (hat * kg[...]).astype(BF16)
 
     span = 2 * HEAD
+    firsts = range(0, groups * RESP, span)
+    blocks = [(s, pl.ds(first, span), first) for s in range(2) for first in firsts]
 
     def response_keys(h):
-        @pl.loop(0, 2)
-        def _(s):
-            pick = jnp.clip(lax.rem(dp + n_dp - rown[s], n_dp), 1, 4)
-            rows = response_rows(s)
-            wide_k, inverse = normed_rows(near[h][pick, pl.ds(0, PROMPT)])
+        normed, bias, keep = [], [], []
+        for s in range(2):
+            wide_k, inverse = normed_rows(near[h][picks[s], pl.ds(0, PROMPT)])
             hat = wide_k * inverse
             r_khat[h, s, pl.ds(0, PROMPT)] = hat
             r_k[h, s, pl.ds(0, PROMPT)] = (hat * kg[...]).astype(BF16)
-            wide_k, inverse = normed_rows(kself[rows, cols(h)])
-            hat = wide_k * inverse
-            r_khat[h, s, pl.ds(PROMPT, RESP)] = hat
-            r_k[h, s, pl.ds(PROMPT, RESP)] = (hat * kg[...]).astype(BF16)
-            normed = r_k[h, s]
-            r_kt[h, s] = dot_nt(eye[...], normed).astype(BF16)
-            owner_length = near_k0[pick, pl.ds(PROMPT, 16)].astype(F32)[0:1]
+            normed.append(r_k[h, s])
+            owner_length = near_k0[picks[s], pl.ds(PROMPT, 16)].astype(F32)[0:1]
             at = lax.broadcasted_iota(jnp.int32, (PROMPT, HEAD), 0).astype(F32)
-            bias = jnp.where(at < owner_length, 0.0, MASKED)
-            bias = jnp.concatenate([bias, bias_own[...]], axis=0)
-            bias = jnp.concatenate([bias, bias], axis=1)
+            seen = jnp.where(at < owner_length, 0.0, MASKED)
+            seen = jnp.concatenate([seen, bias_own[...]], axis=0)
+            bias.append(jnp.concatenate([seen, seen], axis=1))
             place = lax.rem(lax.broadcasted_iota(jnp.int32, (1, span), 1), RESP)
-            keep = (place < rlen[s]).astype(F32)
-            total = jnp.zeros((KEYS, HEAD), F32)
-            for first in range(0, groups * RESP, span):
-                block = pl.ds(first, span)
-                scores = dot_nn(normed, r_qnt[h, s, :, block]) + bias
-                (probs,) = softmax_columns([scores], keep)
-                r_p[h, s, :, block] = probs
-                total = total + dot_nn(probs.astype(BF16), r_o[h, s, block])
-            r_dv[h, s] = total
+            keep.append((place < rlen[s]).astype(F32))
+        scores = [dot_nn(normed[s], r_qnt[h, s, :, b]) + bias[s] for s, b, _ in blocks]
+        probs = [softmax_columns([x], keep[s])[0] for (s, _, _), x in zip(blocks, scores)]
+        weights = [p.astype(BF16) for p in probs]
+        terms = [dot_nn(w, r_o[h, s, b]) for (s, b, _), w in zip(blocks, weights)]
+        for (s, b, _), p in zip(blocks, probs):
+            r_p[h, s, :, b] = p
+        half_way = len(terms) // 2
+        totals = [sum(terms[:half_way]), sum(terms[half_way:])]
+        give_back(heads + h, totals)
+        for s in range(2):
+            dv_out[response_rows(s), cols(h)] = totals[s][PROMPT:].astype(BF16)
+            r_kt[h, s] = dot_nt(eye[...], normed[s]).astype(BF16)
 
     def response_values(h):
-        @pl.loop(0, 2)
-        def _(s):
-            pick = jnp.clip(lax.rem(dp + n_dp - rown[s], n_dp), 1, 4)
+        rows_v = [
+            jnp.concatenate([near[heads + h][picks[s]], vself[response_rows(s), cols(h)]], axis=0)
+            for s in range(2)
+        ]
+        p_grad = [dot_nt(rows_v[s], r_o[h, s, b]) for s, b, _ in blocks]
+        probs = [r_p[h, s, :, b] for s, b, _ in blocks]
+        s_grad = [score_gradient([p], [p.astype(BF16)], [g])[0] for p, g in zip(probs, p_grad)]
+        terms = [dot_nt(x, r_qnt[h, s, :, b]) for (s, b, _), x in zip(blocks, s_grad)]
+        half_way = len(terms) // 2
+        totals = [sum(terms[:half_way]), sum(terms[half_way:])]
+        give_back(h, totals)
+        grads = [dot_nn(r_kt[h, s], x) for (s, _, _), x in zip(blocks, s_grad)]
+        portions = []
+        for (s, b, first), grad in zip(blocks, grads):
+            out, portion = query_backward(grad, r_qt[h, s, :, b], r_inv[h, s, 0:1, b])
+            portions.append(portion)
+            for i in range(span // RESP):
+                dqv[response_rows(s), cols(h, first // RESP + i)] = out[i * RESP : (i + 1) * RESP]
+        qg_acc[...] += sum(portions)
+        portion = sum(totals[s] * r_khat[h, s] for s in range(2)) * SCALE
+        kg_acc[...] += jnp.sum(portion.reshape(KEYS // 8, 8, HEAD), axis=0)
+        for s in range(2):
             rows = response_rows(s)
-            r_v[pl.ds(0, PROMPT)] = near[heads + h][pick]
-            r_v[pl.ds(PROMPT, RESP)] = vself[rows, cols(h)]
-            total = jnp.zeros((KEYS, HEAD), F32)
-            for first in range(0, groups * RESP, span):
-                block = pl.ds(first, span)
-                probs = r_p[h, s, :, block]
-                p_grad = dot_nt(r_v[...], r_o[h, s, block])
-                (s_grad,) = score_gradient([probs], [probs.astype(BF16)], [p_grad])
-                total = total + dot_nt(s_grad, r_qnt[h, s, :, block])
-                grad = dot_nn(r_kt[h, s], s_grad)
-                out = query_backward(grad, r_qt[h, s, :, block], r_inv[h, s, 0:1, block])
-                for i in range(span // RESP):
-                    dqv[rows, cols(h, first // RESP + i)] = out[i * RESP : (i + 1) * RESP]
-            r_dk[h, s] = total
-            portion = total * r_khat[h, s] * SCALE
-            kg_acc[...] += jnp.sum(portion.reshape(KEYS // 8, 8, HEAD), axis=0)
+            dk_out[rows, cols(h)] = key_backward(totals[s][PROMPT:], kself[rows, cols(h)])
 
     def key_backward(grad, rows):
         wide_k, inverse = normed_rows(rows)
@@ -420,9 +423,8 @@
 
     def give_back(c, terms):
         for i, distance in enumerate((1, 3, 2, 4)):
-            first = (picks[0] == distance).astype(F32)
-            second = (picks[1] == distance).astype(F32)
-            term = first * terms[0, pl.ds(0, PROMPT)] + second * terms[1, pl.ds(0, PROMPT)]
+            chosen = [(pick == distance).astype(F32) for pick in picks]
+            term = chosen[0] * terms[0][:PROMPT] + chosen[1] * terms[1][:PROMPT]
             back[c, i] = term.astype(BF16)
         back_across(c).start()
 
@@ -500,92 +502,75 @@
     start_a, collect_a, finish_a = exchange(n_a, peer_a, place_a, part_a, buf_a, a_send, a_recv)
     start_b, collect_b, finish_b = exchange(16, peer_b, place_b, part_b, buf_b, b_send, b_recv)
 
+    def prompt_key_portion():
+        for h in range(heads):
+            wide_k, inverse = normed_rows(kself[pl.ds(0, PROMPT), cols(h)])
+            portion = dk_acc[h] * (wide_k * inverse) * SCALE
+            kg_acc[...] += jnp.sum(portion.reshape(PROMPT // 8, 8, HEAD), axis=0)
+
+    def sum_gains():
+        part_a[...] = jnp.concatenate(
+            [
+                jnp.sum(qg_acc[...].T, axis=0, keepdims=True),
+                jnp.sum(kg_acc[...], axis=0, keepdims=True),
+                jnp.zeros((6, HEAD), F32),
+            ],
+            axis=0,
+        )
+
+    prompt = pl.ds(0, PROMPT)
+
+    def finish_values(h):
+        dv_out[prompt, cols(h)] = (dv_acc[h] + taken_back(heads + h)).astype(BF16)
+
+    def finish_keys(h):
+        dk_out[prompt, cols(h)] = key_backward(dk_acc[h] + taken_back(h), kself[prompt, cols(h)])
+
     for c in range(chunks):
         send_own(c)
+    prepare()
     load_k.wait()
     load_v.wait()
     load_q[0].wait()
     load_o[0].wait()
     prepare_prompt_keys(0)
-    prompt_units(0, 0, groups)
+    prompt_head(0)
     load_q[1].wait()
     load_o[1].wait()
-    prepare_prompt_keys(1)
-    pass_on(0)
     prepare_responses(0)
     prepare_responses(1)
+    pass_on(0)
+    prepare_prompt_keys(1)
+    prompt_head(1)
     pass_on(1)
-    prompt_units(1, 0, 3)
+    prompt_key_portion()
     pass_on(2)
-    prompt_units(1, 3, 6)
     pass_on(3)
-    prompt_units(1, 6, groups)
-    stores = [
-        pltpu.make_async_copy(
-            dqv.at[pl.ds(0, PROMPT)], dq_hbm.at[pl.ds(0, PROMPT)], store_sem.at[0]
-        )
-    ]
-    stores[0].start()
-    for h in range(heads):
-        portion = jnp.zeros((8, HEAD), F32)
-        wide_k, inverse = normed_rows(kself[pl.ds(0, PROMPT), cols(h)])
-        portion = dk_acc[h] * (wide_k * inverse) * SCALE
-        kg_acc[...] += jnp.sum(portion.reshape(PROMPT // 8, 8, HEAD), axis=0)
-
     arrive(0)
     response_keys(0)
-    give_back(2, r_dv.at[0])
     arrive(1)
     response_keys(1)
-    give_back(3, r_dv.at[1])
     give_back_far(2)
     arrive(2)
     response_values(0)
-    give_back(0, r_dk.at[0])
     give_back_far(3)
     arrive(3)
     response_values(1)
-    give_back(1, r_dk.at[1])
-    part_a[...] = jnp.concatenate(
-        [
-            jnp.sum(qg_acc[...].T, axis=0, keepdims=True),
-            jnp.sum(kg_acc[...], axis=0, keepdims=True),
-            jnp.zeros((6, HEAD), F32),
-        ],
-        axis=0,
-    )
+    sum_gains()
     start_a()
     give_back_far(0)
     give_back_far(1)
-    stores.append(
-        pltpu.make_async_copy(
-            dqv.at[pl.ds(PROMPT, 2 * RESP)], dq_hbm.at[pl.ds(PROMPT, 2 * RESP)], store_sem.at[1]
-        )
-    )
-    stores[1].start()
     give_back_near(2)
     give_back_near(3)
     give_back_near(0)
-    for h in range(heads):
-        for s in range(2):
-            rows = pl.ds(PROMPT + s * RESP, RESP)
-            dv_out[rows, cols(h)] = r_dv[h, s, pl.ds(PROMPT, RESP)].astype(BF16)
-            dk_out[rows, cols(h)] = key_backward(
-                r_dk[h, s, pl.ds(PROMPT, RESP)], kself[rows, cols(h)]
-            )
     part_b[...] = collect_a()
     start_b()
     give_back_near(1)
-    prompt = pl.ds(0, PROMPT)
     for h in range(heads):
-        dv_out[prompt, cols(h)] = (dv_acc[h] + taken_back(heads + h)).astype(BF16)
+        finish_values(h)
     for h in range(heads):
-        dk_out[prompt, cols(h)] = key_backward(
-            dk_acc[h] + taken_back(h), kself[prompt, cols(h)]
-        )
-    sums = collect_b()
-    qg_out[...] = sums[0:1]
-    kg_out[...] = sums[1:2]
+        finish_keys(h)
+    gains_out[...] = collect_b()
 
     finish_a()
     finish_b()
@@ -597,7 +582,24 @@
         back_across(c).wait_send()
         back_far(c).wait_send()
         back_near(c).wait_send()
-    for copy in stores:
+
+
+def hand_out(q, k, v, gains, q_out, k_out, v_out, qg_out, kg_out, sems):
+    copies = [
+        pltpu.make_async_copy(src, dst, sems.at[i])
+        for i, (src, dst) in enumerate(
+            [
+                (q, q_out),
+                (k, k_out),
+                (v, v_out),
+                (gains.at[0:1], qg_out),
+                (gains.at[1:2], kg_out),
+            ]
+        )
+    ]
+    for copy in copies:
+        copy.start()
+    for copy in copies:
         copy.wait()
 
 
@@ -616,7 +618,6 @@
     scratch = [
         pltpu.VMEM(queries.shape, BF16),
         pltpu.VMEM(queries.shape, BF16),
-        pltpu.VMEM(queries.shape, BF16),
         pltpu.VMEM(keys.shape, BF16),
         pltpu.VMEM(keys.shape, BF16),
         pltpu.VMEM((5, PROMPT + 16, HEAD), BF16),
@@ -625,6 +626,7 @@
         pltpu.VMEM((5, PROMPT, HEAD), BF16),
         pltpu.VMEM((HEAD, HEAD), BF16),
         pltpu.VMEM((HEAD, HEAD), F32),
+        pltpu.VMEM((PROMPT // 2, PROMPT), F32),
         pltpu.VMEM((PROMPT, PROMPT), F32),
         pltpu.VMEM((RESP, HEAD), F32),
         pltpu.VMEM((heads, PROMPT, HEAD), BF16),
@@ -641,9 +643,6 @@
         pltpu.VMEM((heads, 2, HEAD, KEYS), BF16),
         pltpu.VMEM((heads, 2, KEYS, HEAD), F32),
         pltpu.VMEM((heads, 2, KEYS, asked), F32),
-        pltpu.VMEM((KEYS, HEAD), BF16),
-        pltpu.VMEM((heads, 2, KEYS, HEAD), F32),
-        pltpu.VMEM((heads, 2, KEYS, HEAD), F32),
         pltpu.VMEM((chunks, 4, PROMPT, HEAD), BF16),
         pltpu.VMEM((chunks, 2, PROMPT, HEAD), BF16),
         pltpu.VMEM((chunks, PROMPT, HEAD), BF16),
@@ -655,7 +654,6 @@
         pltpu.VMEM((n_a, 8, HEAD), F32),
         pltpu.VMEM((16, 8, HEAD), F32),
         pltpu.SemaphoreType.DMA((chunks + 2 + 2 * heads,)),
-        pltpu.SemaphoreType.DMA((2,)),
         pltpu.SemaphoreType.DMA((4, chunks)),
         pltpu.SemaphoreType.DMA((4, chunks)),
         pltpu.SemaphoreType.DMA((3, chunks)),
@@ -665,17 +663,16 @@
         pltpu.SemaphoreType.DMA((16,)),
         pltpu.SemaphoreType.DMA((16,)),
     ]
-    q_grad, k_grad, v_grad, q_gain_grad, k_gain_grad = pl.pallas_call(
+    results = pl.pallas_call(
         functools.partial(kernel, heads, groups, n_dp, n_tensor),
         out_shape=(
-            jax.ShapeDtypeStruct(queries.shape, BF16),
-            jax.ShapeDtypeStruct(keys.shape, BF16),
-            jax.ShapeDtypeStruct(keys.shape, BF16),
-            jax.ShapeDtypeStruct((1, HEAD), F32),
-            jax.ShapeDtypeStruct((1, HEAD), F32),
+            pltpu.VMEM(queries.shape, BF16),
+            pltpu.VMEM(keys.shape, BF16),
+            pltpu.VMEM(keys.shape, BF16),
+            pltpu.VMEM((8, HEAD), F32),
         ),
         in_specs=[smem, smem, smem, vmem, vmem, hbm, hbm, hbm, hbm],
-        out_specs=(hbm, vmem, vmem, vmem, vmem),
+        out_specs=(vmem, vmem, vmem, vmem),
         scratch_shapes=scratch,
         compiler_params=pltpu.CompilerParams(
             collective_id=0, has_side_effects=True, vmem_limit_bytes=56 * 2**20
@@ -687,11 +684,25 @@
         resp_owner,
         q_gain.reshape(1, HEAD),
         k_gain.reshape(1, HEAD),
-        queries,
-        keys,
-        values,
-        output_gradient,
+        *[
+            pltpu.with_memory_space_constraint(a, pltpu.HBM)
+            for a in (queries, keys, values, output_gradient)
+        ],
     )
+    q_grad, k_grad, v_grad, q_gain_grad, k_gain_grad = pl.pallas_call(
+        hand_out,
+        out_shape=(
+            jax.ShapeDtypeStruct(queries.shape, BF16),
+            jax.ShapeDtypeStruct(keys.shape, BF16),
+            jax.ShapeDtypeStruct(keys.shape, BF16),
+            jax.ShapeDtypeStruct((1, HEAD), F32),
+            jax.ShapeDtypeStruct((1, HEAD), F32),
+        ),
+        in_specs=[vmem] * 4,
+        out_specs=(hbm,) * 5,
+        scratch_shapes=[pltpu.SemaphoreType.DMA((5,))],
+        name="hand_out",
+    )(*results)
     return q_grad, k_grad, v_grad, q_gain_grad.reshape(HEAD), k_gain_grad.reshape(HEAD)
 
 

time: 56.1 us -> 48.5 us (0.86)
  the two profiles are of different devices: /device:TPU:1 before, /device:TPU:5 now
where the time goes in v2:
time: 48.5 us; the launch traced here: 48.4 us
  Pallas kernels  44 us (91%)
  local copies, waits for them, and re-layouts  3.1 us (6%)
  between operations  1.3 us (3%)
    pallas_call x1, Pallas kernels, on_device(): pl.pallas_call(functools.partial(kernel, heads, groups, n_dp, n_tensor),...  41.2 us
    unnamed x8, local copies, waits for them, and re-layouts  3.1 us
    pallas_call x1, Pallas kernels, on_device(): pl.pallas_call(hand_out, out_shape=(jax.ShapeDtypeStruct(queries.shape, B...  2.83 us

profile of v2, /device:TPU:5, one launch (start us, length us, event | category | flops | bytes accessed | tf_op | source)
XLA Modules:
  0.0 48.4 jit_solution(3233171297730442932)
XLA Ops:
  1.3 41.2 %attention.1 = (bf16[384,2048]{1,0:T(8,128)(2,1)S(1)}, bf16[384,256]{1,0:T(8,128)(2,1)S(1)}, bf16[384,256]{1,0:T(8,128)(2,1)S(1)}, f32[8,128]{1,0:T(8,128)S(1)}) custom-call(s32[1]{0:T(128)S(6)} %copy.14.plen, s32[2]{0:T(128)} %rlen.1, s32[2]{0:T(128)} %rown.1, f32[1,128]{1,0:T(1,128)} %bitcast.4, f32[1,128]{1,0:T(1,128)} %bitcast.5, ...), custom_call_target="tpu_custom_call" | custom-call | tf_op jit(solution)/shard_map/attention/pallas_call | solution.py:666
  42.4 0.0 copy-start
  42.4 1.1 %copy-done = bf16[384,2048]{1,0:T(8,128)(2,1)} copy-done((bf16[384,2048]{1,0:T(8,128)(2,1)}, bf16[384,2048]{1,0:T(8,128)(2,1)S(1)}, u32[]{:S(2)}) %copy-start) | copy-done | bytes 1572888
  43.6 0.0 copy-start.1
  43.6 0.7 %copy-done.1 = bf16[384,256]{1,0:T(8,128)(2,1)} copy-done((bf16[384,256]{1,0:T(8,128)(2,1)}, bf16[384,256]{1,0:T(8,128)(2,1)S(1)}, u32[]{:S(2)}) %copy-start.1) | copy-done | bytes 196632
  44.3 0.0 copy-start.2
  44.3 0.7 %copy-done.2 = bf16[384,256]{1,0:T(8,128)(2,1)} copy-done((bf16[384,256]{1,0:T(8,128)(2,1)}, bf16[384,256]{1,0:T(8,128)(2,1)S(1)}, u32[]{:S(2)}) %copy-start.2) | copy-done | bytes 196632
  45.0 0.0 copy-start.3
  45.0 0.6 %copy-done.3 = f32[8,128]{1,0:T(8,128)} copy-done((f32[8,128]{1,0:T(8,128)}, f32[8,128]{1,0:T(8,128)S(1)}, u32[]{:S(2)}) %copy-start.3) | copy-done | bytes 4120
  45.6 2.8 %hand_out.1 = (bf16[384,2048]{1,0:T(8,128)(2,1)}, bf16[384,256]{1,0:T(8,128)(2,1)}, bf16[384,256]{1,0:T(8,128)(2,1)}, f32[1,128]{1,0:T(1,128)}, f32[1,128]{1,0:T(1,128)}) custom-call(bf16[384,2048]{1,0:T(8,128)(2,1)} %copy-done, bf16[384,256]{1,0:T(8,128)(2,1)} %copy-done.1, bf16[384,256]{1,0:T(8,128)(2,1)} %copy-done.2, f32[8,128]{1,0:T(8,128)} %copy-done.3), custom_call_target="tpu_custom_call" | custom-call | tf_op jit(solution)/shard_map/hand_out/pallas_call | solution.py:692
Async XLA Ops:
  42.4 1.2 %copy-start = (bf16[384,2048]{1,0:T(8,128)(2,1)}, bf16[384,2048]{1,0:T(8,128)(2,1)S(1)}, u32[]{:S(2)}) copy-start(bf16[384,2048]{1,0:T(8,128)(2,1)S(1)} %get-tuple-element.14.q) | copy-start | bytes 4718596
  43.6 0.7 %copy-start.1 = (bf16[384,256]{1,0:T(8,128)(2,1)}, bf16[384,256]{1,0:T(8,128)(2,1)S(1)}, u32[]{:S(2)}) copy-start(bf16[384,256]{1,0:T(8,128)(2,1)S(1)} %get-tuple-element.15.k) | copy-start | bytes 589828
  44.3 0.7 %copy-start.2 = (bf16[384,256]{1,0:T(8,128)(2,1)}, bf16[384,256]{1,0:T(8,128)(2,1)S(1)}, u32[]{:S(2)}) copy-start(bf16[384,256]{1,0:T(8,128)(2,1)S(1)} %get-tuple-element.16.v) | copy-start | bytes 589828
  45.0 0.6 %copy-start.3 = (f32[8,128]{1,0:T(8,128)}, f32[8,128]{1,0:T(8,128)S(1)}, u32[]{:S(2)}) copy-start(f32[8,128]{1,0:T(8,128)S(1)} %get-tuple-element.17.gains) | copy-start | bytes 12292

commit v3 on v2

--- a/solution.py
+++ b/solution.py
@@ -76,6 +76,7 @@
     gains_out,
     qv,
     ov,
+    length_at,
     kself,
     vself,
     near_k0,
@@ -126,6 +127,8 @@
     core = lax.rem(dp, 2)
     up = (lax.rem(dp + 2, n_dp), tensor)
     down = (lax.rem(dp + n_dp - 2, n_dp), tensor)
+    far_up = (lax.rem(dp + 4, n_dp), tensor)
+    far_down = (lax.rem(dp + n_dp - 4, n_dp), tensor)
     sibling = (dp + 1 - 2 * core, tensor)
     near = (near_k0, near_k1, near_v0, near_v1)
     chunks = 2 * heads
@@ -135,13 +138,20 @@
     place_a = lax.div(dp, 16) * n_tensor + tensor
     place_b = lax.rem(dp, 16)
 
-    def peer_a(k):
-        place = lax.rem(place_a + k, n_a)
-        return place, (lax.div(place, n_tensor) * 16 + place_b, lax.rem(place, n_tensor))
-
-    def peer_b(k):
-        place = lax.rem(place_b + k, 16)
-        return place, (dp - place_b + place, tensor)
+    def within(at, size):
+        return jnp.where(at < size, at, at - size)
+
+    column = lax.div(dp, 16)
+    peers_a = []
+    for i in range(columns):
+        for j in range(n_tensor):
+            if i or j:
+                at, side = within(column + i, columns), within(tensor + j, n_tensor)
+                peers_a.append((at * n_tensor + side, (at * 16 + place_b, side)))
+    peers_b = []
+    for k in range(1, 16):
+        at = within(place_b + k, 16)
+        peers_b.append((at, (dp - place_b + at, tensor)))
 
     def cols(h, g=None):
         if g is None:
@@ -161,6 +171,7 @@
         h = c % heads
         source = (k_hbm if c < heads else v_hbm).at[pl.ds(0, PROMPT), cols(h)]
         staged.append(load(source, near[c].at[0, pl.ds(0, PROMPT)]))
+    load_length = load(plen, length_at)
     load_k = load(k_hbm, kself)
     wide = groups * HEAD
     load_q, load_o = [], []
@@ -171,20 +182,12 @@
             load_v = load(v_hbm, vself)
 
     barrier = pltpu.get_barrier_semaphore()
-    for neighbour in (up, down):
-        pl.semaphore_signal(barrier, inc=1, device_id=neighbour, device_id_type=MESH)
-
-    @pl.loop(1, 16)
-    def _(k):
-        pl.semaphore_signal(barrier, inc=1, device_id=peer_b(k)[1], device_id_type=MESH)
-
-    if n_a > 1:
-
-        @pl.loop(1, n_a)
-        def _(k):
-            pl.semaphore_signal(barrier, inc=1, device_id=peer_a(k)[1], device_id_type=MESH)
-
-    length = plen[0]
+    greeted = [up, down, far_up, far_down] + [device for _, device in peers_b + peers_a]
+    for device in greeted:
+        pl.semaphore_signal(barrier, inc=1, device_id=device, device_id_type=MESH)
+
+    load_length.wait()
+    length = length_at[0]
     query_at = lax.rem(lax.broadcasted_iota(jnp.int32, (1, PROMPT), 1), PROMPT // 2)
     keep_lower = (query_at < length).astype(F32)
     keep_upper = (query_at + PROMPT // 2 < length).astype(F32)
@@ -212,7 +215,7 @@
 
     for copy in staged:
         copy.wait()
-    pl.semaphore_wait(barrier, 2 + 15 + n_a - 1)
+    pl.semaphore_wait(barrier, len(greeted))
 
     def slot(c, d):
         return near[c].at[d]
@@ -418,6 +421,9 @@
     def back_far(c):
         return backward(1, c, back_o4.at[c], back_r4.at[c], down)
 
+    def back_direct(c):
+        return backward(1, c, back_o4.at[c], back_r4.at[c], far_down)
+
     def back_near(c):
         return backward(2, c, back_o2.at[c], back_r2.at[c], down)
 
@@ -443,64 +449,55 @@
         back_o2[c] = total.astype(BF16)
         back_near(c).start()
 
-    def taken_back(c):
+    def give_back_direct(c):
+        back_across(c).wait_recv()
+        total = back[c, 3].astype(F32) + upper * back_sib[c, 1].astype(F32)
+        back_o4[c] = total.astype(BF16)
+        back_direct(c).start()
+        other = upper * back_sib[c, 0].astype(F32) + (1.0 - upper) * back_sib[c, 1].astype(F32)
+        back_o2[c] = (back[c, 2].astype(F32) + other).astype(BF16)
+        back_near(c).start()
+
+    def taken_back(c, direct=False):
         back_near(c).wait_recv()
-        return back_r2[c].astype(F32) + (1.0 - upper) * back_sib[c, 0].astype(F32)
-
-    def exchange(n, peer, place, source, buffer, send_sem, recv_sem):
-        def copy(k):
-            other, device = peer(k)
+        total = back_r2[c].astype(F32) + (1.0 - upper) * back_sib[c, 0].astype(F32)
+        if direct:
+            back_direct(c).wait_recv()
+            total = total + back_r4[c].astype(F32)
+        return total
+
+    def exchange(peers, place, source, buffer, send_sem, recv_sem):
+        def copy(other, device, slot):
             return pltpu.make_async_remote_copy(
                 src_ref=source,
-                dst_ref=buffer.at[place],
+                dst_ref=buffer.at[slot],
                 send_sem=send_sem.at[other],
-                recv_sem=recv_sem.at[place],
+                recv_sem=recv_sem.at[slot],
                 device_id=device,
                 device_id_type=MESH,
             )
 
-        def arriving(k):
-            other, device = peer(k)
-            return pltpu.make_async_remote_copy(
-                src_ref=source,
-                dst_ref=buffer.at[other],
-                send_sem=send_sem.at[other],
-                recv_sem=recv_sem.at[other],
-                device_id=device,
-                device_id_type=MESH,
-            )
-
         def start():
-            if n > 1:
-
-                @pl.loop(1, n)
-                def _(k):
-                    copy(k).start()
+            for other, device in peers:
+                copy(other, device, place).start()
+            buffer[place] = source[...]
 
         def collect():
-            buffer[place] = source[...]
-            if n > 1:
-
-                @pl.loop(1, n)
-                def _(k):
-                    arriving(k).wait_recv()
-
+            for other, device in peers:
+                copy(other, device, other).wait_recv()
             total = buffer[0]
-            for i in range(1, n):
+            for i in range(1, len(peers) + 1):
                 total = total + buffer[i]
             return total
 
         def finish():
-            if n > 1:
-
-                @pl.loop(1, n)
-                def _(k):
-                    copy(k).wait_send()
+            for other, device in peers:
+                copy(other, device, place).wait_send()
 
         return start, collect, finish
 
-    start_a, collect_a, finish_a = exchange(n_a, peer_a, place_a, part_a, buf_a, a_send, a_recv)
-    start_b, collect_b, finish_b = exchange(16, peer_b, place_b, part_b, buf_b, b_send, b_recv)
+    start_a, collect_a, finish_a = exchange(peers_b, place_b, part_b, buf_b, b_send, b_recv)
+    start_b, collect_b, finish_b = exchange(peers_a, place_a, part_a, buf_a, a_send, a_recv)
 
     def prompt_key_portion():
         for h in range(heads):
@@ -509,7 +506,7 @@
             kg_acc[...] += jnp.sum(portion.reshape(PROMPT // 8, 8, HEAD), axis=0)
 
     def sum_gains():
-        part_a[...] = jnp.concatenate(
+        part_b[...] = jnp.concatenate(
             [
                 jnp.sum(qg_acc[...].T, axis=0, keepdims=True),
                 jnp.sum(kg_acc[...], axis=0, keepdims=True),
@@ -524,7 +521,8 @@
         dv_out[prompt, cols(h)] = (dv_acc[h] + taken_back(heads + h)).astype(BF16)
 
     def finish_keys(h):
-        dk_out[prompt, cols(h)] = key_backward(dk_acc[h] + taken_back(h), kself[prompt, cols(h)])
+        total = dk_acc[h] + taken_back(h)
+        dk_out[prompt, cols(h)] = key_backward(total, kself[prompt, cols(h)])
 
     for c in range(chunks):
         send_own(c)
@@ -562,9 +560,9 @@
     give_back_far(1)
     give_back_near(2)
     give_back_near(3)
+    part_a[...] = collect_a()
+    start_b()
     give_back_near(0)
-    part_b[...] = collect_a()
-    start_b()
     give_back_near(1)
     for h in range(heads):
         finish_values(h)
@@ -618,6 +616,7 @@
     scratch = [
         pltpu.VMEM(queries.shape, BF16),
         pltpu.VMEM(queries.shape, BF16),
+        pltpu.SMEM((1,), jnp.int32),
         pltpu.VMEM(keys.shape, BF16),
         pltpu.VMEM(keys.shape, BF16),
         pltpu.VMEM((5, PROMPT + 16, HEAD), BF16),
@@ -653,7 +652,7 @@
         pltpu.VMEM((8, HEAD), F32),
         pltpu.VMEM((n_a, 8, HEAD), F32),
         pltpu.VMEM((16, 8, HEAD), F32),
-        pltpu.SemaphoreType.DMA((chunks + 2 + 2 * heads,)),
+        pltpu.SemaphoreType.DMA((chunks + 3 + 2 * heads,)),
         pltpu.SemaphoreType.DMA((4, chunks)),
         pltpu.SemaphoreType.DMA((4, chunks)),
         pltpu.SemaphoreType.DMA((3, chunks)),
@@ -671,7 +670,7 @@
             pltpu.VMEM(keys.shape, BF16),
             pltpu.VMEM((8, HEAD), F32),
         ),
-        in_specs=[smem, smem, smem, vmem, vmem, hbm, hbm, hbm, hbm],
+        in_specs=[hbm, smem, smem, vmem, vmem, hbm, hbm, hbm, hbm],
         out_specs=(vmem, vmem, vmem, vmem),
         scratch_shapes=scratch,
         compiler_params=pltpu.CompilerParams(
@@ -701,8 +700,9 @@
         in_specs=[vmem] * 4,
         out_specs=(hbm,) * 5,
         scratch_shapes=[pltpu.SemaphoreType.DMA((5,))],
+        compiler_params=pltpu.CompilerParams(vmem_limit_bytes=16 * 2**20),
         name="hand_out",
-    )(*results)
+    )(*[pltpu.with_memory_space_constraint(x, pltpu.VMEM) for x in results])
     return q_grad, k_grad, v_grad, q_gain_grad.reshape(HEAD), k_gain_grad.reshape(HEAD)
 
 

time: 48.5 us -> 42.5 us (0.88)
  the two profiles are of different devices: /device:TPU:5 before, /device:TPU:1 now
where the time goes in v3:
time: 42.5 us; the launch traced here: 42.4 us
  Pallas kernels  41.1 us (97%)
  between operations  1.29 us (3%)
    pallas_call x1, Pallas kernels, on_device(): pl.pallas_call(functools.partial(kernel, heads, groups, n_dp, n_tensor),...  39.8 us
    pallas_call x1, Pallas kernels, on_device(): pl.pallas_call(hand_out, out_shape=(jax.ShapeDtypeStruct(queries.shape, B...  1.31 us

profile of v3, /device:TPU:1, one launch (start us, length us, event | category | flops | bytes accessed | tf_op | source)
XLA Modules:
  0.0 42.4 jit_solution(17981107423977505863)
XLA Ops:
  1.3 39.8 %attention.1 = (bf16[384,2048]{1,0:T(8,128)(2,1)S(1)}, bf16[384,256]{1,0:T(8,128)(2,1)S(1)}, bf16[384,256]{1,0:T(8,128)(2,1)S(1)}, f32[8,128]{1,0:T(8,128)S(1)}) custom-call(s32[1]{0:T(128)S(6)} %copy.14.plen, s32[2]{0:T(128)} %rlen.1, s32[2]{0:T(128)} %rown.1, f32[1,128]{1,0:T(1,128)} %bitcast.4, f32[1,128]{1,0:T(1,128)} %bitcast.5, ...), custom_call_target="tpu_custom_call" | custom-call | tf_op jit(solution)/shard_map/attention/pallas_call | solution.py:665
  41.1 1.3 %hand_out.1 = (bf16[384,2048]{1,0:T(8,128)(2,1)}, bf16[384,256]{1,0:T(8,128)(2,1)}, bf16[384,256]{1,0:T(8,128)(2,1)}, f32[1,128]{1,0:T(1,128)}, f32[1,128]{1,0:T(1,128)}) custom-call(bf16[384,2048]{1,0:T(8,128)(2,1)S(1)} %get-tuple-element.14.q, bf16[384,256]{1,0:T(8,128)(2,1)S(1)} %get-tuple-element.15.k, bf16[384,256]{1,0:T(8,128)(2,1)S(1)} %get-tuple-element.16.v, ...), custom_call_target="tpu_custom_call" | custom-call | tf_op jit(solution)/shard_map/hand_out/pallas_call | solution.py:691

commit v4 on v3

--- a/solution.py
+++ b/solution.py
@@ -112,6 +112,7 @@
     part_b,
     buf_a,
     buf_b,
+    known,
     load_sem,
     fwd_send,
     fwd_recv,
@@ -127,8 +128,6 @@
     core = lax.rem(dp, 2)
     up = (lax.rem(dp + 2, n_dp), tensor)
     down = (lax.rem(dp + n_dp - 2, n_dp), tensor)
-    far_up = (lax.rem(dp + 4, n_dp), tensor)
-    far_down = (lax.rem(dp + n_dp - 4, n_dp), tensor)
     sibling = (dp + 1 - 2 * core, tensor)
     near = (near_k0, near_k1, near_v0, near_v1)
     chunks = 2 * heads
@@ -157,6 +156,19 @@
         if g is None:
             return pl.ds(h * HEAD, HEAD)
         return pl.ds(pl.multiple_of((h * groups + g) * HEAD, HEAD), HEAD)
+
+    barrier = pltpu.get_barrier_semaphore()
+    rings = [
+        (dp - place_b + within(place_b + 2, 16), tensor),
+        (dp - place_b + within(place_b + 14, 16), tensor),
+    ]
+    if n_tensor > 1:
+        rings += [(dp, within(tensor + j, n_tensor)) for j in (1, n_tensor - 1)]
+    if columns > 1:
+        rings += [(within(column + i, columns) * 16 + place_b, tensor) for i in (1, columns - 1)]
+    greeted = [up, down, sibling] + rings
+    for device in greeted:
+        pl.semaphore_signal(barrier, inc=1, device_id=device, device_id_type=MESH)
 
     loads = []
 
@@ -180,11 +192,6 @@
         load_o.append(load(o_hbm.at[:, pl.ds(h * wide, wide)], ov.at[:, pl.ds(h * wide, wide)]))
         if h == 0:
             load_v = load(v_hbm, vself)
-
-    barrier = pltpu.get_barrier_semaphore()
-    greeted = [up, down, far_up, far_down] + [device for _, device in peers_b + peers_a]
-    for device in greeted:
-        pl.semaphore_signal(barrier, inc=1, device_id=device, device_id_type=MESH)
 
     load_length.wait()
     length = length_at[0]
@@ -217,6 +224,16 @@
         copy.wait()
     pl.semaphore_wait(barrier, len(greeted))
 
+    def tell(turn):
+        for i, device in enumerate(rings):
+            pl.semaphore_signal(
+                known.at[turn, i], inc=1, device_id=device, device_id_type=MESH
+            )
+
+    def hear(turn):
+        for i in range(len(rings)):
+            pl.semaphore_wait(known.at[turn, i], 1)
+
     def slot(c, d):
         return near[c].at[d]
 
@@ -292,10 +309,10 @@
 
     half = PROMPT // 2
 
-    def prompt_head(h):
+    def prompt_half(h, pairs):
         lo, hi = pl.ds(0, half), pl.ds(half, half)
         parts = []
-        for pair in range(groups // 2):
+        for pair in pairs:
             at = [cols(h, 2 * pair + i) for i in range(2)]
             parts.append((at, lo, lo, bias_lower, keep_lower))
             parts.append((at, hi, pl.ds(0, PROMPT), bias_upper, keep_upper))
@@ -421,9 +438,6 @@
     def back_far(c):
         return backward(1, c, back_o4.at[c], back_r4.at[c], down)
 
-    def back_direct(c):
-        return backward(1, c, back_o4.at[c], back_r4.at[c], far_down)
-
     def back_near(c):
         return backward(2, c, back_o2.at[c], back_r2.at[c], down)
 
@@ -449,22 +463,9 @@
         back_o2[c] = total.astype(BF16)
         back_near(c).start()
 
-    def give_back_direct(c):
-        back_across(c).wait_recv()
-        total = back[c, 3].astype(F32) + upper * back_sib[c, 1].astype(F32)
-        back_o4[c] = total.astype(BF16)
-        back_direct(c).start()
-        other = upper * back_sib[c, 0].astype(F32) + (1.0 - upper) * back_sib[c, 1].astype(F32)
-        back_o2[c] = (back[c, 2].astype(F32) + other).astype(BF16)
-        back_near(c).start()
-
-    def taken_back(c, direct=False):
+    def taken_back(c):
         back_near(c).wait_recv()
-        total = back_r2[c].astype(F32) + (1.0 - upper) * back_sib[c, 0].astype(F32)
-        if direct:
-            back_direct(c).wait_recv()
-            total = total + back_r4[c].astype(F32)
-        return total
+        return back_r2[c].astype(F32) + (1.0 - upper) * back_sib[c, 0].astype(F32)
 
     def exchange(peers, place, source, buffer, send_sem, recv_sem):
         def copy(other, device, slot):
@@ -524,26 +525,35 @@
         total = dk_acc[h] + taken_back(h)
         dk_out[prompt, cols(h)] = key_backward(total, kself[prompt, cols(h)])
 
-    for c in range(chunks):
-        send_own(c)
+    first, second = range(groups // 4), range(groups // 4, groups // 2)
+    send_own(0)
+    tell(0)
     prepare()
     load_k.wait()
     load_v.wait()
-    load_q[0].wait()
-    load_o[0].wait()
-    prepare_prompt_keys(0)
-    prompt_head(0)
-    load_q[1].wait()
-    load_o[1].wait()
-    prepare_responses(0)
-    prepare_responses(1)
+    for h in range(heads):
+        load_q[h].wait()
+        load_o[h].wait()
+        prepare_prompt_keys(h)
+        prepare_responses(h)
+    send_own(1)
+    prompt_half(0, first)
+    send_own(2)
+    prompt_half(0, second)
+    hear(0)
+    tell(1)
+    prompt_half(1, first)
     pass_on(0)
-    prepare_prompt_keys(1)
-    prompt_head(1)
+    send_own(3)
+    prompt_half(1, second)
+    hear(1)
+    tell(2)
     pass_on(1)
     prompt_key_portion()
     pass_on(2)
     pass_on(3)
+    hear(2)
+    tell(3)
     arrive(0)
     response_keys(0)
     arrive(1)
@@ -555,6 +565,7 @@
     arrive(3)
     response_values(1)
     sum_gains()
+    hear(3)
     start_a()
     give_back_far(0)
     give_back_far(1)
@@ -587,7 +598,7 @@
         pltpu.make_async_copy(src, dst, sems.at[i])
         for i, (src, dst) in enumerate(
             [
-                (q, q_out),
+                *[(q.at[r], q_out.at[r]) for r in (pl.ds(96 * i, 96) for i in range(4))],
                 (k, k_out),
                 (v, v_out),
                 (gains.at[0:1], qg_out),
@@ -652,6 +663,7 @@
         pltpu.VMEM((8, HEAD), F32),
         pltpu.VMEM((n_a, 8, HEAD), F32),
         pltpu.VMEM((16, 8, HEAD), F32),
+        pltpu.SemaphoreType.REGULAR((4, 6)),
         pltpu.SemaphoreType.DMA((chunks + 3 + 2 * heads,)),
         pltpu.SemaphoreType.DMA((4, chunks)),
         pltpu.SemaphoreType.DMA((4, chunks)),
@@ -699,7 +711,7 @@
         ),
         in_specs=[vmem] * 4,
         out_specs=(hbm,) * 5,
-        scratch_shapes=[pltpu.SemaphoreType.DMA((5,))],
+        scratch_shapes=[pltpu.SemaphoreType.DMA((8,))],
         compiler_params=pltpu.CompilerParams(vmem_limit_bytes=16 * 2**20),
         name="hand_out",
     )(*[pltpu.with_memory_space_constraint(x, pltpu.VMEM) for x in results])

time: 42.5 us -> 41.4 us (0.974)
  Pallas kernels: 41.1 us -> 40 us
    pallas_call x1, Pallas kernels: 39.8 us -> 38.7 us  [on_device(): pl.pallas_call(functools.partial(kernel, heads, groups, n_dp, n_tensor),...]
where the time goes in v4:
time: 41.4 us; the launch traced here: 41.3 us
  Pallas kernels  40 us (97%)
  between operations  1.29 us (3%)
    pallas_call x1, Pallas kernels, on_device(): pl.pallas_call(functools.partial(kernel, heads, groups, n_dp, n_tensor),...  38.7 us
    pallas_call x1, Pallas kernels, on_device(): pl.pallas_call(hand_out, out_shape=(jax.ShapeDtypeStruct(queries.shape, B...  1.34 us

profile of v4, /device:TPU:1, one launch (start us, length us, event | category | flops | bytes accessed | tf_op | source)
XLA Modules:
  0.0 41.3 jit_solution(9874733491019562397)
XLA Ops:
  1.3 38.7 %attention.1 = (bf16[384,2048]{1,0:T(8,128)(2,1)S(1)}, bf16[384,256]{1,0:T(8,128)(2,1)S(1)}, bf16[384,256]{1,0:T(8,128)(2,1)S(1)}, f32[8,128]{1,0:T(8,128)S(1)}) custom-call(s32[1]{0:T(128)S(6)} %copy.14.plen, s32[2]{0:T(128)} %rlen.1, s32[2]{0:T(128)} %rown.1, f32[1,128]{1,0:T(1,128)} %bitcast.4, f32[1,128]{1,0:T(1,128)} %bitcast.5, ...), custom_call_target="tpu_custom_call" | custom-call | tf_op jit(solution)/shard_map/attention/pallas_call | solution.py:677
  39.9 1.3 %hand_out.1 = (bf16[384,2048]{1,0:T(8,128)(2,1)}, bf16[384,256]{1,0:T(8,128)(2,1)}, bf16[384,256]{1,0:T(8,128)(2,1)}, f32[1,128]{1,0:T(1,128)}, f32[1,128]{1,0:T(1,128)}) custom-call(bf16[384,2048]{1,0:T(8,128)(2,1)S(1)} %get-tuple-element.14.q, bf16[384,256]{1,0:T(8,128)(2,1)S(1)} %get-tuple-element.15.k, bf16[384,256]{1,0:T(8,128)(2,1)S(1)} %get-tuple-element.16.v, ...), custom_call_target="tpu_custom_call" | custom-call | tf_op jit(solution)/shard_map/hand_out/pallas_call | solution.py:703

commit v5 on v4

--- a/solution.py
+++ b/solution.py
@@ -526,7 +526,8 @@
         dk_out[prompt, cols(h)] = key_backward(total, kself[prompt, cols(h)])
 
     first, second = range(groups // 4), range(groups // 4, groups // 2)
-    send_own(0)
+    for c in range(chunks):
+        send_own(c)
     tell(0)
     prepare()
     load_k.wait()
@@ -536,15 +537,12 @@
         load_o[h].wait()
         prepare_prompt_keys(h)
         prepare_responses(h)
-    send_own(1)
     prompt_half(0, first)
-    send_own(2)
     prompt_half(0, second)
     hear(0)
     tell(1)
     prompt_half(1, first)
     pass_on(0)
-    send_own(3)
     prompt_half(1, second)
     hear(1)
     tell(2)

time: 41.4 us -> 40.9 us (0.988)
  Pallas kernels: 40 us -> 39.5 us
    pallas_call x1, Pallas kernels: 38.7 us -> 38.1 us  [on_device(): pl.pallas_call(functools.partial(kernel, heads, groups, n_dp, n_tensor),...]
where the time goes in v5:
time: 40.9 us; the launch traced here: 40.8 us
  Pallas kernels  39.5 us (97%)
  between operations  1.29 us (3%)
    pallas_call x1, Pallas kernels, on_device(): pl.pallas_call(functools.partial(kernel, heads, groups, n_dp, n_tensor),...  38.1 us
    pallas_call x1, Pallas kernels, on_device(): pl.pallas_call(hand_out, out_shape=(jax.ShapeDtypeStruct(queries.shape, B...  1.34 us

profile of v5, /device:TPU:1, one launch (start us, length us, event | category | flops | bytes accessed | tf_op | source)
XLA Modules:
  0.0 40.8 jit_solution(8575001038716321422)
XLA Ops:
  1.3 38.1 %attention.1 = (bf16[384,2048]{1,0:T(8,128)(2,1)S(1)}, bf16[384,256]{1,0:T(8,128)(2,1)S(1)}, bf16[384,256]{1,0:T(8,128)(2,1)S(1)}, f32[8,128]{1,0:T(8,128)S(1)}) custom-call(s32[1]{0:T(128)S(6)} %copy.14.plen, s32[2]{0:T(128)} %rlen.1, s32[2]{0:T(128)} %rown.1, f32[1,128]{1,0:T(1,128)} %bitcast.4, f32[1,128]{1,0:T(1,128)} %bitcast.5, ...), custom_call_target="tpu_custom_call" | custom-call | tf_op jit(solution)/shard_map/attention/pallas_call | solution.py:675
  39.4 1.3 %hand_out.1 = (bf16[384,2048]{1,0:T(8,128)(2,1)}, bf16[384,256]{1,0:T(8,128)(2,1)}, bf16[384,256]{1,0:T(8,128)(2,1)}, f32[1,128]{1,0:T(1,128)}, f32[1,128]{1,0:T(1,128)}) custom-call(bf16[384,2048]{1,0:T(8,128)(2,1)S(1)} %get-tuple-element.14.q, bf16[384,256]{1,0:T(8,128)(2,1)S(1)} %get-tuple-element.15.k, bf16[384,256]{1,0:T(8,128)(2,1)S(1)} %get-tuple-element.16.v, ...), custom_call_target="tpu_custom_call" | custom-call | tf_op jit(solution)/shard_map/hand_out/pallas_call | solution.py:701

commit v6 on v5

--- a/solution.py
+++ b/solution.py
@@ -573,14 +573,7 @@
     start_b()
     give_back_near(0)
     give_back_near(1)
-    for h in range(heads):
-        finish_values(h)
-    for h in range(heads):
-        finish_keys(h)
-    gains_out[...] = collect_b()
-
     finish_a()
-    finish_b()
     for c in range(chunks):
         hop(c).wait_send()
         relay(c).wait_send()
@@ -588,7 +581,17 @@
         across(c, 1, 0).wait_send()
         back_across(c).wait_send()
         back_far(c).wait_send()
+    for c in range(heads, chunks):
         back_near(c).wait_send()
+    for h in range(heads):
+        finish_values(h)
+    for h in range(heads):
+        finish_keys(h)
+    gains_out[...] = collect_b()
+
+    finish_b()
+    back_near(0).wait_send()
+    back_near(1).wait_send()
 
 
 def hand_out(q, k, v, gains, q_out, k_out, v_out, qg_out, kg_out, sems):

time: 40.9 us -> 40.8 us (level)
  no operation moved by 1% of the time
where the time goes in v6:
time: 40.8 us; the launch traced here: 40.7 us
  Pallas kernels  39.5 us (97%)
  between operations  1.29 us (3%)
    pallas_call x1, Pallas kernels, on_device(): pl.pallas_call(functools.partial(kernel, heads, groups, n_dp, n_tensor),...  38.1 us
    pallas_call x1, Pallas kernels, on_device(): pl.pallas_call(hand_out, out_shape=(jax.ShapeDtypeStruct(queries.shape, B...  1.34 us

profile of v6, /device:TPU:1, one launch (start us, length us, event | category | flops | bytes accessed | tf_op | source)
XLA Modules:
  0.0 40.7 jit_solution(3824568543432685651)
XLA Ops:
  1.3 38.1 %attention.1 = (bf16[384,2048]{1,0:T(8,128)(2,1)S(1)}, bf16[384,256]{1,0:T(8,128)(2,1)S(1)}, bf16[384,256]{1,0:T(8,128)(2,1)S(1)}, f32[8,128]{1,0:T(8,128)S(1)}) custom-call(s32[1]{0:T(128)S(6)} %copy.14.plen, s32[2]{0:T(128)} %rlen.1, s32[2]{0:T(128)} %rown.1, f32[1,128]{1,0:T(1,128)} %bitcast.4, f32[1,128]{1,0:T(1,128)} %bitcast.5, ...), custom_call_target="tpu_custom_call" | custom-call | tf_op jit(solution)/shard_map/attention/pallas_call | solution.py:678
  39.4 1.3 %hand_out.1 = (bf16[384,2048]{1,0:T(8,128)(2,1)}, bf16[384,256]{1,0:T(8,128)(2,1)}, bf16[384,256]{1,0:T(8,128)(2,1)}, f32[1,128]{1,0:T(1,128)}, f32[1,128]{1,0:T(1,128)}) custom-call(bf16[384,2048]{1,0:T(8,128)(2,1)S(1)} %get-tuple-element.14.q, bf16[384,256]{1,0:T(8,128)(2,1)S(1)} %get-tuple-element.15.k, bf16[384,256]{1,0:T(8,128)(2,1)S(1)} %get-tuple-element.16.v, ...), custom_call_target="tpu_custom_call" | custom-call | tf_op jit(solution)/shard_map/hand_out/pallas_call | solution.py:704
